TPU v7x, 256 devices: a whole 4x4x8 slice. The times are simulated.
256 devices in a mesh: lat: 32 (over z, x_lo, core), krylov: 8 (over x_hi, y).
Axes of the slice: x: 4 (x_hi: 2, x_lo: 2; x = x_hi * 2 + x_lo), y: 4, z: 8, core: 2. Of those that a mesh axis runs over, the one named last changes fastest.
Arguments:
- start_block: bfloat16 [32, 4, 16, 2, 400], P('lat'), may hold values from -6 to 6
- self_block: bfloat16 [32, 4, 2, 400, 400], P('lat'), may hold values from -1 to 1, as said below
- hop_links: bfloat16 [32, 4, 2, 2, 400, 400], P('lat'), may hold values from -0.078125 to 0.078125
- stored_vectors: bfloat16 [1024, 32, 4, 2, 400], P('krylov', 'lat'), may hold values from -0.01953125 to 0.01953125
Outputs:
- filtered_block: bfloat16 [32, 4, 16, 2, 400], P('lat')
- coefficients: float32 [1024, 2, 16], P('krylov')
Inputs may be any that keep to these rules, and one draw needn't show every extreme that they name: `self_block`: each site's block is Hermitian: its real part is symmetric and its imaginary part antisymmetric.
All inputs are finite; a program needn't handle non-finite values.
Results may differ from a plain program's by a relative error of at most 0.024.
Values may be sent and summed in bfloat16 or wider, within the bound.
A program may use at most 128 MiB of HBM per device.

v0:
```python
import jax
import jax.numpy as jnp
from jax import lax
from jax.sharding import PartitionSpec as P

DEG = 6


CENTER = 0.25
HALF_WIDTH = 3.25


def from_behind(array, axis, by):
    count = lax.axis_size(axis)
    return lax.ppermute(array, axis, [(i, (i + by) % count) for i in range(count)])


def forward_hop(link, vector):
    product = jnp.einsum("tsrcb,tsdab->tsrcda", vector, link, preferred_element_type=jnp.float32)
    real_part = product[..., 0, 0, :] - product[..., 1, 1, :]
    imag_part = product[..., 1, 0, :] + product[..., 0, 1, :]
    return jnp.stack([real_part, imag_part], axis=3)


def adjoint_hop(link, vector):
    product = jnp.einsum("tsrcb,tsdba->tsrcda", vector, link, preferred_element_type=jnp.float32)
    real_part = product[..., 0, 0, :] + product[..., 1, 1, :]
    imag_part = product[..., 1, 0, :] - product[..., 0, 1, :]
    return jnp.stack([real_part, imag_part], axis=3)


def pairing(stored):
    count = stored.shape[0]
    flat = stored.reshape(count, -1)
    turned = jnp.stack([-stored[..., 1, :], stored[..., 0, :]], axis=3).reshape(count, -1)
    return (flat, jnp.concatenate([flat, turned], axis=0))


def coefficient_terms(vectors_flat, block):
    rounded = block.astype(jnp.bfloat16)
    turned = jnp.stack([rounded[..., 1, :], -rounded[..., 0, :]], axis=3)
    joined = jnp.concatenate([rounded, turned], axis=2)
    rows = jnp.transpose(joined, (2, 0, 1, 3, 4)).reshape(joined.shape[2], -1)
    return lax.dot_general(
        vectors_flat, rows, (((1,), (1,)), ((), ())), preferred_element_type=jnp.float32
    )


def correction(paired_flat, coefs, block_shape):
    width = coefs.shape[1] // 2
    rounded = coefs.astype(jnp.bfloat16)
    stacked = jnp.concatenate([rounded[:, :width], rounded[:, width:]], axis=0)
    terms = lax.dot_general(
        paired_flat, stacked, (((0,), (0,)), ((), ())), preferred_element_type=jnp.float32
    )
    terms = terms.reshape(
        block_shape[0], block_shape[1], block_shape[3], block_shape[4], block_shape[2]
    )
    return jnp.transpose(terms, (0, 1, 4, 2, 3))


def shards(start_block, self_block, hop_links, stored_vectors):
    x_links = hop_links[:, :, 0]
    t_links = hop_links[:, :, 1]

    def behind(rounded):
        return from_behind(adjoint_hop(t_links, rounded), "lat", 1)

    def operate(rounded):
        total = forward_hop(self_block, rounded)
        total = total + forward_hop(x_links, jnp.roll(rounded, -1, axis=1))
        total = total + jnp.roll(adjoint_hop(x_links, rounded), 1, axis=1)
        ahead = from_behind(rounded, "lat", -1)
        total = total + forward_hop(t_links, ahead)
        return total + behind(rounded)

    def chebyshev(start):
        previous = start
        current = (operate(start.astype(jnp.bfloat16)) - CENTER * start) / HALF_WIDTH
        for degree_step in range(DEG - 1):
            image = operate(current.astype(jnp.bfloat16))
            following = 2.0 / HALF_WIDTH * (image - CENTER * current) - previous
            previous, current = (current, following)
        return current

    block = chebyshev(chebyshev(start_block.astype(jnp.float32)))
    kry_local = stored_vectors.shape[0]
    vectors_flat, paired_flat = pairing(stored_vectors)
    total = jnp.zeros((kry_local, 2 * block.shape[2]), jnp.float32)
    for pass_index in range(2):
        coefs = lax.psum(coefficient_terms(vectors_flat, block), "lat")
        total = total + coefs
        block = block - lax.psum(
            correction(paired_flat, coefs, block.shape).astype(jnp.bfloat16), "krylov"
        ).astype(jnp.float32)
    coefficients = total.reshape(kry_local, 2, block.shape[2])
    return (block.astype(jnp.bfloat16), coefficients)


def solution(mesh):
    placed = (
        P("lat", None, None, None, None),
        P("lat", None, None, None, None),
        P("lat", None, None, None, None, None),
        P("krylov", "lat", None, None, None),
    )
    return jax.shard_map(
        shards,
        mesh=mesh,
        in_specs=placed,
        out_specs=(P("lat", None, None, None, None), P("krylov", None, None)),
        check_vma=False,
    )
```

profile of v0, /device:TPU:32, one launch (start us, length us, event | category | flops | bytes accessed | tf_op | source)
XLA Modules:
  0.0 567.8 jit_solution(13294417026041469840)
XLA Ops:
  7.2 1.1 copy.137
  8.9 3.3 slice_bitcast_fusion.1
  18.1 1.7 collective-permute-done.1
  25.8 5.3 collective-permute-done.3
  36.9 7.8 %collective-permute-done.5 = f32[1,4,16,2,400]{4,2,1,3,0:T(8,128)S(1)} collective-permute-done((f32[1,4,16,2,400]{4,2,1,3,0:T(8,128)S(1)}, f32[1,4,16,2,400]{4,2,1,3,0:T(8,128)S(1)}, u32[]{:S(2)}, u32[]{:S(2)}) %collective-permute-start.5) | collective-permute-done | bytes 204832 | tf_op jit(solution)/shard_map/ppermute | solution.py:15
  50.1 7.1 %collective-permute-done.7 = f32[1,4,16,2,400]{4,2,1,3,0:T(8,128)S(1)} collective-permute-done((f32[1,4,16,2,400]{4,2,1,3,0:T(8,128)S(1)}, f32[1,4,16,2,400]{4,2,1,3,0:T(8,128)S(1)}, u32[]{:S(2)}, u32[]{:S(2)}) %collective-permute-start.7) | collective-permute-done | bytes 204832 | tf_op jit(solution)/shard_map/ppermute | solution.py:15
  58.8 1.0 convolution_bitcast_fusion.39
  62.6 6.3 %collective-permute-done.9 = f32[1,4,16,2,400]{4,2,1,3,0:T(8,128)S(1)} collective-permute-done((f32[1,4,16,2,400]{4,2,1,3,0:T(8,128)S(1)}, f32[1,4,16,2,400]{4,2,1,3,0:T(8,128)S(1)}, u32[]{:S(2)}, u32[]{:S(2)}) %collective-permute-start.9) | collective-permute-done | bytes 204832 | tf_op jit(solution)/shard_map/ppermute | solution.py:15
  70.5 1.0 convolution_bitcast_fusion.34
  74.5 6.3 %collective-permute-done.11 = f32[1,4,16,2,400]{4,2,1,3,0:T(8,128)S(1)} collective-permute-done((f32[1,4,16,2,400]{4,2,1,3,0:T(8,128)S(1)}, f32[1,4,16,2,400]{4,2,1,3,0:T(8,128)S(1)}, u32[]{:S(2)}, u32[]{:S(2)}) %collective-permute-start.11) | collective-permute-done | bytes 204832 | tf_op jit(solution)/shard_map/ppermute | solution.py:15
  86.3 6.3 %collective-permute-done.13 = f32[1,4,16,2,400]{4,2,1,3,0:T(8,128)S(1)} collective-permute-done((f32[1,4,16,2,400]{4,2,1,3,0:T(8,128)S(1)}, f32[1,4,16,2,400]{4,2,1,3,0:T(8,128)S(1)}, u32[]{:S(2)}, u32[]{:S(2)}) %collective-permute-start.13) | collective-permute-done | bytes 204832 | tf_op jit(solution)/shard_map/ppermute | solution.py:15
  98.0 6.3 %collective-permute-done.15 = f32[1,4,16,2,400]{4,2,1,3,0:T(8,128)S(1)} collective-permute-done((f32[1,4,16,2,400]{4,2,1,3,0:T(8,128)S(1)}, f32[1,4,16,2,400]{4,2,1,3,0:T(8,128)S(1)}, u32[]{:S(2)}, u32[]{:S(2)}) %collective-permute-start.15) | collective-permute-done | bytes 204832 | tf_op jit(solution)/shard_map/ppermute | solution.py:15
  109.9 6.3 %collective-permute-done.17 = f32[1,4,16,2,400]{4,2,1,3,0:T(8,128)S(1)} collective-permute-done((f32[1,4,16,2,400]{4,2,1,3,0:T(8,128)S(1)}, f32[1,4,16,2,400]{4,2,1,3,0:T(8,128)S(1)}, u32[]{:S(2)}, u32[]{:S(2)}) %collective-permute-start.17) | collective-permute-done | bytes 204832 | tf_op jit(solution)/shard_map/ppermute | solution.py:15
  117.9 1.0 convolution_bitcast_fusion.14
  121.7 6.3 %collective-permute-done.19 = f32[1,4,16,2,400]{4,2,1,3,0:T(8,128)S(1)} collective-permute-done((f32[1,4,16,2,400]{4,2,1,3,0:T(8,128)S(1)}, f32[1,4,16,2,400]{4,2,1,3,0:T(8,128)S(1)}, u32[]{:S(2)}, u32[]{:S(2)}) %collective-permute-start.19) | collective-permute-done | bytes 204832 | tf_op jit(solution)/shard_map/ppermute | solution.py:15
  129.6 1.0 convolution_bitcast_fusion.9
  133.4 6.3 %collective-permute-done.21 = f32[1,4,16,2,400]{4,2,1,3,0:T(8,128)S(1)} collective-permute-done((f32[1,4,16,2,400]{4,2,1,3,0:T(8,128)S(1)}, f32[1,4,16,2,400]{4,2,1,3,0:T(8,128)S(1)}, u32[]{:S(2)}, u32[]{:S(2)}) %collective-permute-start.21) | collective-permute-done | bytes 204832 | tf_op jit(solution)/shard_map/ppermute | solution.py:15
  141.4 1.0 convolution_bitcast_fusion.4
  145.4 6.3 %collective-permute-done.23 = f32[1,4,16,2,400]{4,2,1,3,0:T(8,128)S(1)} collective-permute-done((f32[1,4,16,2,400]{4,2,1,3,0:T(8,128)S(1)}, f32[1,4,16,2,400]{4,2,1,3,0:T(8,128)S(1)}, u32[]{:S(2)}, u32[]{:S(2)}) %collective-permute-start.23) | collective-permute-done | bytes 204832 | tf_op jit(solution)/shard_map/ppermute | solution.py:15
  152.9 103.1 %psum.28 = f32[128,32]{0,1:T(8,128)S(1)} all-reduce(f32[128,32]{0,1:T(8,128)} %convolution_bitcast_fusion.60), channel_id=1, replica_groups=mesh['lat'=32,'krylov'=8] {'lat'}, use_global_device_ids=true, to_apply=%region_0.1 | all-reduce | flops 4096 | bytes 32768 | tf_op jit(solution)/shard_map/psum | solution.py:91
  256.0 2.6 convolution_convert_fusion.1
  258.6 1.8 convert_element_type.91
  260.4 1.6 copy.648
  262.1 93.5 %all-reduce.3.cloned.1.call-done = bf16[1,4,16,2,400]{4,2,1,3,0:T(8,128)(2,1)} async-done(((bf16[1,4,16,2,400]{4,2,1,3,0:T(8,128)(2,1)}), bf16[1,4,16,2,400]{4,2,1,3,0:T(8,128)(2,1)}) %all-reduce.3.cloned.1.call-update) | async-done | bytes 102416 | tf_op jit(solution)/shard_map/psum | solution.py:93
  356.5 2.0 convolution_bitcast_fusion.59
  358.6 97.6 %psum.30 = f32[128,32]{0,1:T(8,128)} all-reduce(f32[128,32]{0,1:T(8,128)} %convolution_bitcast_fusion.59), channel_id=1, replica_groups=mesh['lat'=32,'krylov'=8] {'lat'}, use_global_device_ids=true, to_apply=%region_2.3 | all-reduce | flops 4096 | bytes 32768 | tf_op jit(solution)/shard_map/psum | solution.py:91
  456.2 1.4 fusion.382
  457.6 2.6 convolution_convert_fusion
  460.1 1.8 convert_element_type.97
  462.0 1.6 copy.647
  463.6 95.1 %all-reduce.5.cloned.1.call-done = bf16[1,4,16,2,400]{4,2,1,3,0:T(8,128)(2,1)} async-done(((bf16[1,4,16,2,400]{4,2,1,3,0:T(8,128)(2,1)}), bf16[1,4,16,2,400]{4,2,1,3,0:T(8,128)(2,1)}) %all-reduce.5.cloned.1.call-update) | async-done | bytes 102416 | tf_op jit(solution)/shard_map/psum | solution.py:93
  558.7 1.0 subtract_convert_fusion
  (218 shorter events, 64.6 us)
Async XLA Ops:
  7.2 6.6 %copy-start = (bf16[1,4,2,400,400]{4,3,2,1,0:T(8,128)(2,1)S(1)}, bf16[1,4,2,400,400]{4,3,2,1,0:T(8,128)(2,1)}, u32[]{:S(2)}) copy-start(bf16[1,4,2,400,400]{4,3,2,1,0:T(8,128)(2,1)} %param.5) | copy-start | bytes 7680004
  7.2 348.4 %all-reduce.3.cloned.1.call-start = ((), (), s32[]{:S(2)}) async-start(), calls=%async_computation | async-start | bytes 262144 | tf_op jit(solution)/shard_map/psum | solution.py:93
  8.3 3.9 copy-start.1
  8.3 8.7 %collective-permute-start = (bf16[1,4,16,2,400]{4,2,3,1,0:T(8,128)(2,1)S(1)}, bf16[1,4,16,2,400]{4,2,3,1,0:T(8,128)(2,1)S(1)}, u32[]{:S(2)}, u32[]{:S(2)}) collective-permute-start(bf16[1,4,16,2,400]{4,2,3,1,0:T(8,128)(2,1)S(1)} %copy.137), channel_id=1, source_target_pairs={{0,248},{8,0},{16,8},{24,16},{32,24},{40,32},{48,40},{56,48},{64,5... | collective-permute-start | bytes 307208 | tf_op jit(solution)/shard_map/ppermute | solution.py:15
  13.0 6.8 %collective-permute-start.1 = (f32[1,4,16,2,400]{4,2,1,3,0:T(8,128)S(1)}, f32[1,4,16,2,400]{4,2,1,3,0:T(8,128)S(1)}, u32[]{:S(2)}, u32[]{:S(2)}) collective-permute-start(f32[1,4,16,2,400]{4,2,1,3,0:T(8,128)S(1)} %pad_maximum_fusion.28), channel_id=1, source_target_pairs={{0,8},{8,16},{16,24},{24,32},{32,40},{40,48},{48,56},{56,64},{64,7... | collective-permute-start | bytes 614408 | tf_op jit(solution)/shard_map/ppermute | solution.py:15
  14.8 1.2 copy-start.2
  21.3 3.5 collective-permute-start.2
  24.4 6.8 %collective-permute-start.3 = (f32[1,4,16,2,400]{4,2,1,3,0:T(8,128)S(1)}, f32[1,4,16,2,400]{4,2,1,3,0:T(8,128)S(1)}, u32[]{:S(2)}, u32[]{:S(2)}) collective-permute-start(f32[1,4,16,2,400]{4,2,1,3,0:T(8,128)S(1)} %pad_maximum_fusion.29), channel_id=1, source_target_pairs={{0,8},{8,16},{16,24},{24,32},{32,40},{40,48},{48,56},{56,64},{64,7... | collective-permute-start | bytes 614408 | tf_op jit(solution)/shard_map/ppermute | solution.py:15
  32.0 3.8 collective-permute-start.4
  34.9 9.8 %collective-permute-start.5 = (f32[1,4,16,2,400]{4,2,1,3,0:T(8,128)S(1)}, f32[1,4,16,2,400]{4,2,1,3,0:T(8,128)S(1)}, u32[]{:S(2)}, u32[]{:S(2)}) collective-permute-start(f32[1,4,16,2,400]{4,2,1,3,0:T(8,128)S(1)} %pad_maximum_fusion.30), channel_id=1, source_target_pairs={{0,8},{8,16},{16,24},{24,32},{32,40},{40,48},{48,56},{56,64},{64,7... | collective-permute-start | bytes 614408 | tf_op jit(solution)/shard_map/ppermute | solution.py:15
  45.6 3.5 collective-permute-start.6
  48.5 8.8 %collective-permute-start.7 = (f32[1,4,16,2,400]{4,2,1,3,0:T(8,128)S(1)}, f32[1,4,16,2,400]{4,2,1,3,0:T(8,128)S(1)}, u32[]{:S(2)}, u32[]{:S(2)}) collective-permute-start(f32[1,4,16,2,400]{4,2,1,3,0:T(8,128)S(1)} %pad_maximum_fusion.31), channel_id=1, source_target_pairs={{0,8},{8,16},{16,24},{24,32},{32,40},{40,48},{48,56},{56,64},{64,7... | collective-permute-start | bytes 614408 | tf_op jit(solution)/shard_map/ppermute | solution.py:15
  58.1 3.5 collective-permute-start.8
  61.0 8.0 %collective-permute-start.9 = (f32[1,4,16,2,400]{4,2,1,3,0:T(8,128)S(1)}, f32[1,4,16,2,400]{4,2,1,3,0:T(8,128)S(1)}, u32[]{:S(2)}, u32[]{:S(2)}) collective-permute-start(f32[1,4,16,2,400]{4,2,1,3,0:T(8,128)S(1)} %pad_maximum_fusion.32), channel_id=1, source_target_pairs={{0,8},{8,16},{16,24},{24,32},{32,40},{40,48},{48,56},{56,64},{64,7... | collective-permute-start | bytes 614408 | tf_op jit(solution)/shard_map/ppermute | solution.py:15
  69.8 3.6 collective-permute-start.10
  72.7 8.2 %collective-permute-start.11 = (f32[1,4,16,2,400]{4,2,1,3,0:T(8,128)S(1)}, f32[1,4,16,2,400]{4,2,1,3,0:T(8,128)S(1)}, u32[]{:S(2)}, u32[]{:S(2)}) collective-permute-start(f32[1,4,16,2,400]{4,2,1,3,0:T(8,128)S(1)} %pad_maximum_fusion.33), channel_id=1, source_target_pairs={{0,8},{8,16},{16,24},{24,32},{32,40},{40,48},{48,56},{56,64},{64,7... | collective-permute-start | bytes 614408 | tf_op jit(solution)/shard_map/ppermute | solution.py:15
  81.8 3.5 collective-permute-start.12
  84.6 8.0 %collective-permute-start.13 = (f32[1,4,16,2,400]{4,2,1,3,0:T(8,128)S(1)}, f32[1,4,16,2,400]{4,2,1,3,0:T(8,128)S(1)}, u32[]{:S(2)}, u32[]{:S(2)}) collective-permute-start(f32[1,4,16,2,400]{4,2,1,3,0:T(8,128)S(1)} %pad_maximum_fusion.34), channel_id=1, source_target_pairs={{0,8},{8,16},{16,24},{24,32},{32,40},{40,48},{48,56},{56,64},{64,7... | collective-permute-start | bytes 614408 | tf_op jit(solution)/shard_map/ppermute | solution.py:15
  93.5 3.5 collective-permute-start.14
  96.3 8.0 %collective-permute-start.15 = (f32[1,4,16,2,400]{4,2,1,3,0:T(8,128)S(1)}, f32[1,4,16,2,400]{4,2,1,3,0:T(8,128)S(1)}, u32[]{:S(2)}, u32[]{:S(2)}) collective-permute-start(f32[1,4,16,2,400]{4,2,1,3,0:T(8,128)S(1)} %pad_maximum_fusion.35), channel_id=1, source_target_pairs={{0,8},{8,16},{16,24},{24,32},{32,40},{40,48},{48,56},{56,64},{64,7... | collective-permute-start | bytes 614408 | tf_op jit(solution)/shard_map/ppermute | solution.py:15
  105.2 3.7 collective-permute-start.16
  108.1 8.2 %collective-permute-start.17 = (f32[1,4,16,2,400]{4,2,1,3,0:T(8,128)S(1)}, f32[1,4,16,2,400]{4,2,1,3,0:T(8,128)S(1)}, u32[]{:S(2)}, u32[]{:S(2)}) collective-permute-start(f32[1,4,16,2,400]{4,2,1,3,0:T(8,128)S(1)} %pad_maximum_fusion.36), channel_id=1, source_target_pairs={{0,8},{8,16},{16,24},{24,32},{32,40},{40,48},{48,56},{56,64},{64,7... | collective-permute-start | bytes 614408 | tf_op jit(solution)/shard_map/ppermute | solution.py:15
  117.2 3.5 collective-permute-start.18
  120.0 8.0 %collective-permute-start.19 = (f32[1,4,16,2,400]{4,2,1,3,0:T(8,128)S(1)}, f32[1,4,16,2,400]{4,2,1,3,0:T(8,128)S(1)}, u32[]{:S(2)}, u32[]{:S(2)}) collective-permute-start(f32[1,4,16,2,400]{4,2,1,3,0:T(8,128)S(1)} %pad_maximum_fusion.37), channel_id=1, source_target_pairs={{0,8},{8,16},{16,24},{24,32},{32,40},{40,48},{48,56},{56,64},{64,7... | collective-permute-start | bytes 614408 | tf_op jit(solution)/shard_map/ppermute | solution.py:15
  128.9 3.5 collective-permute-start.20
  131.8 8.0 %collective-permute-start.21 = (f32[1,4,16,2,400]{4,2,1,3,0:T(8,128)S(1)}, f32[1,4,16,2,400]{4,2,1,3,0:T(8,128)S(1)}, u32[]{:S(2)}, u32[]{:S(2)}) collective-permute-start(f32[1,4,16,2,400]{4,2,1,3,0:T(8,128)S(1)} %pad_maximum_fusion.38), channel_id=1, source_target_pairs={{0,8},{8,16},{16,24},{24,32},{32,40},{40,48},{48,56},{56,64},{64,7... | collective-permute-start | bytes 614408 | tf_op jit(solution)/shard_map/ppermute | solution.py:15
  140.7 3.7 collective-permute-start.22
  143.5 8.2 %collective-permute-start.23 = (f32[1,4,16,2,400]{4,2,1,3,0:T(8,128)S(1)}, f32[1,4,16,2,400]{4,2,1,3,0:T(8,128)S(1)}, u32[]{:S(2)}, u32[]{:S(2)}) collective-permute-start(f32[1,4,16,2,400]{4,2,1,3,0:T(8,128)S(1)} %pad_maximum_fusion.39), channel_id=1, source_target_pairs={{0,8},{8,16},{16,24},{24,32},{32,40},{40,48},{48,56},{56,64},{64,7... | collective-permute-start | bytes 614408 | tf_op jit(solution)/shard_map/ppermute | solution.py:15
  262.1 296.7 %all-reduce.5.cloned.1.call-start = ((), (), s32[]{:S(2)}) async-start(), calls=%async_computation.1 | async-start | bytes 262144 | tf_op jit(solution)/shard_map/psum | solution.py:93
Sparse Core Ops, SparseCore 0:
  262.2 93.3 all-reduce.2
  463.7 94.9 all-reduce.4
where the time goes:
time: 577 us; the launch traced here: 568 us
  waiting for transfers between devices  261 us (45%)
  blocking collectives  201 us (35%)
  matrix products  59.6 us (10%)
  between operations  15.5 us (3%)
  local copies, waits for them, and re-layouts  12.3 us (2%)
  other arithmetic  9.43 us (2%)
  starting transfers between devices  8.78 us (2%)
    psum x2, blocking collectives, shards(): coefs = lax.psum(coefficient_terms(vectors_flat, block), 'lat')  201 us
    psum x2, waiting for transfers between devices, shards(): lax.psum(correction(paired_flat, coefs, block.shape).astype(jnp.bfloat16)...  189 us
    ppermute x24, waiting for transfers between devices, from_behind(): lax.ppermute(array, axis, [(i, (i + by) % count) for i in range(count)])  72.8 us
    dot_general x36, matrix products, forward_hop(): jnp.einsum('tsrcb,tsdab->tsrcda', vector, link, preferred_element_type=jn...  35.5 us
    dot_general x24, matrix products, adjoint_hop(): jnp.einsum('tsrcb,tsdba->tsrcda', vector, link, preferred_element_type=jn...  16 us
  transfers between devices with their start and end apart: 26, of which 15 were waited for; matrix products, arithmetic and copies ran while one was open for 9% of the time, Pallas kernels for 0%

commit v1 on v0

v1 whole, which is shorter than its diff:
```python
import functools

import jax
import jax.numpy as jnp
from jax import lax
from jax.experimental import pallas as pl
from jax.experimental.pallas import tpu as pltpu
from jax.sharding import PartitionSpec as P

MESH = pl.DeviceIdType.MESH
BF16, F32 = jnp.bfloat16, jnp.float32

DEG = 6
CENTER = 0.25
HALF_WIDTH = 3.25

SITES, NB = 4, 400
QUARTER = 4
ROWS = 2 * QUARTER
FLAT = SITES * 2 * NB
GROUP = 128
CHIPS = 16


def dot(x, w):
    return lax.dot_general(x, w, (((1,), (0,)), ((), ())), preferred_element_type=F32)


def dot_t(x, w):
    return lax.dot_general(x, w, (((1,), (1,)), ((), ())), preferred_element_type=F32)


def turn(x):
    half = x.shape[0] // 2
    if x.shape[0] == ROWS:
        return jnp.concatenate([x[half:], -x[:half]], axis=0)
    return jnp.concatenate(
        [turn(x[i : i + ROWS]) for i in range(0, x.shape[0], ROWS)], axis=0
    )


def kernel(
    start_ref, self_hbm, hop_hbm, stored_hbm,
    out_ref, coef_ref,
    self_w, hop_w, ahead_w, stored,
    cur, prev, vsend, vrecv, psend, precv,
    asend, arecv, zbuf, dsend, drecv, ssend, srecv, fbuf, ebuf,
    load_sem, vs_sem, vr_sem, ps_sem, pr_sem, gs_sem, gr_sem,
    as_sem, ar_sem, zs_sem, zr_sem, ds_sem, dr_sem, ss_sem, sr_sem,
    fs_sem, fr_sem, es_sem, er_sem,
):
    lat, kry = lax.axis_index("lat"), lax.axis_index("krylov")
    y, h = lax.rem(kry, 4), kry // 4
    core, chip = lax.rem(lat, 2), lat // 2
    ahead = (lax.rem(lat + 1, 32), kry)
    behind = (lax.rem(lat + 31, 32), kry)
    partner = (chip * 2 + 1 - core, kry)
    sibling = (lat, (1 - h) * 4 + y)

    def ring(j):
        return lax.rem(y + j, 4)

    def along_y(j):
        return (lat, h * 4 + ring(j))

    def other_chip(j):
        return lax.rem(chip + j, CHIPS)

    barrier = pltpu.get_barrier_semaphore()
    greet = [ahead, behind, sibling]
    greet += [along_y(j) for j in (1, 2, 3)]
    greet += [(other_chip(j) * 2 + core, kry) for j in range(1, CHIPS)]
    for device in greet:
        pl.semaphore_signal(barrier, inc=1, device_id=device, device_id_type=MESH)

    def remote(src, dst, send_sem, recv_sem, device):
        return pltpu.make_async_remote_copy(
            src_ref=src, dst_ref=dst, send_sem=send_sem, recv_sem=recv_sem,
            device_id=device, device_id_type=MESH,
        )

    loads = [
        pltpu.make_async_copy(hop_hbm, hop_w, load_sem.at[0]),
        pltpu.make_async_copy(self_hbm, self_w, load_sem.at[1]),
        pltpu.make_async_copy(stored_hbm, stored.at[pl.ds(0, GROUP)], load_sem.at[2]),
    ]
    for load in loads:
        load.start()
    cur[...] = start_ref[...]
    prev[...] = start_ref[...]
    loads[0].wait()
    row = lax.broadcasted_iota(jnp.int32, (NB, NB), 0)
    col = lax.broadcasted_iota(jnp.int32, (NB, NB), 1)
    eye = (row == col).astype(BF16)

    def flip(site, carry):
        ahead_w[site, 0] = dot_t(eye, hop_w[site, 1, 0]).astype(BF16)
        ahead_w[site, 1] = (-dot_t(eye, hop_w[site, 1, 1])).astype(BF16)
        return carry

    lax.fori_loop(0, SITES, flip, 0)
    loads[1].wait()

    pl.semaphore_wait(barrier, len(greet))

    gathers = [
        remote(
            stored_hbm, stored.at[pl.ds(j * GROUP, GROUP)],
            gs_sem.at[j - 1], gr_sem.at[j - 1], along_y(j),
        )
        for j in (1, 2, 3)
    ]
    for gather in gathers:
        gather.start()

    def step(i, carry):
        p = lax.rem(i, 2)
        first = lax.rem(i, DEG) == 0
        scale = jnp.where(first, 1.0 / HALF_WIDTH, 2.0 / HALF_WIDTH).astype(F32)
        keep = jnp.where(first, 0.0, 1.0).astype(F32)
        x = cur[...]
        xb = x.astype(BF16)
        xt = turn(x).astype(BF16)
        vsend[...] = xb
        back = remote(vsend, vrecv.at[p], vs_sem.at[p], vr_sem.at[p], behind)
        back.start()
        parts = []
        for s in range(SITES):
            rows = slice(s * ROWS, s * ROWS + ROWS)
            parts.append(dot(xb[rows], hop_w[s, 1, 0]) + dot(xt[rows], hop_w[s, 1, 1]))
        psend[...] = jnp.concatenate(parts, axis=0).astype(BF16)
        forth = remote(psend, precv.at[p], ps_sem.at[p], pr_sem.at[p], ahead)
        forth.start()
        parts = []
        for s in range(SITES):
            rows = slice(s * ROWS, s * ROWS + ROWS)
            nxt = (s + 1) % SITES
            nrows = slice(nxt * ROWS, nxt * ROWS + ROWS)
            lst = (s - 1) % SITES
            lrows = slice(lst * ROWS, lst * ROWS + ROWS)
            total = dot(xb[rows], self_w[s, 0]) + dot(xt[rows], self_w[s, 1])
            total += dot(xb[lrows], hop_w[lst, 0, 0]) + dot(xt[lrows], hop_w[lst, 0, 1])
            total += dot_t(xb[nrows], hop_w[s, 0, 0]) - dot_t(xt[nrows], hop_w[s, 0, 1])
            parts.append(total)
        here = jnp.concatenate(parts, axis=0)
        base = scale * (here - CENTER * x) - keep * prev[...]
        back.wait_recv()
        vb = vrecv[p]
        vt = turn(vb.astype(F32)).astype(BF16)
        parts = []
        for s in range(SITES):
            rows = slice(s * ROWS, s * ROWS + ROWS)
            parts.append(dot(vb[rows], ahead_w[s, 0]) + dot(vt[rows], ahead_w[s, 1]))
        there = jnp.concatenate(parts, axis=0)
        forth.wait_recv()
        there = there + precv[p].astype(F32)
        prev[...] = x
        cur[...] = base + scale * there
        back.wait_send()
        forth.wait_send()
        return carry

    lax.fori_loop(0, 2 * DEG, step, 0)

    loads[2].wait()
    for gather in gathers:
        gather.wait()

    total = None
    for n in range(2):
        x = cur[...]
        xt = turn(x)
        pieces = []
        for s in range(SITES):
            rows = slice(s * ROWS, s * ROWS + ROWS)
            pieces += [x[rows], xt[rows]]
        flat = jnp.concatenate(pieces, axis=1).astype(BF16)
        part = dot_t(flat, stored[...])
        low, high = part[:, : 2 * GROUP], part[:, 2 * GROUP :]
        asend[n] = jnp.where(core == 0, high, low)
        cross = remote(asend.at[n], arecv.at[n], as_sem.at[n], ar_sem.at[n], partner)
        cross.start()
        mine = jnp.where(core == 0, low, high)
        cross.wait_recv()
        mine = mine + arecv[n]
        zbuf[n, chip] = jnp.concatenate(
            [mine[:, :GROUP], mine[:, GROUP:]], axis=0
        ).astype(BF16)
        sends = []
        for j in (8, 7, 9, 6, 10, 5, 11, 4, 12, 3, 13, 2, 14, 1, 15):
            sends.append(
                remote(
                    zbuf.at[n, chip], zbuf.at[n, chip], zs_sem.at[n, j], zr_sem.at[n, chip],
                    (other_chip(j) * 2 + core, kry),
                )
            )
        for send in sends:
            send.start()
        for j in range(1, CHIPS):
            source = other_chip(j)
            remote(
                zbuf.at[n, source], zbuf.at[n, source], zs_sem.at[n, j], zr_sem.at[n, source],
                (other_chip(j) * 2 + core, kry),
            ).wait_recv()
        summed = zbuf[n, 0].astype(F32)
        for q in range(1, CHIPS):
            summed = summed + zbuf[n, q].astype(F32)
        own = jnp.concatenate([summed[:ROWS], summed[ROWS:]], axis=1)
        dsend[n] = own
        cross_back = remote(dsend.at[n], drecv.at[n], ds_sem.at[n], dr_sem.at[n], partner)
        cross_back.start()
        cross_back.wait_recv()
        other = drecv[n]
        coef = jnp.concatenate(
            [jnp.where(core == 0, own, other), jnp.where(core == 0, other, own)], axis=1
        )
        total = coef if total is None else total + coef
        if n == 1:
            for j in range(4):
                ebuf[0, j] = total[:, j * GROUP : (j + 1) * GROUP]
            coef_sends = [
                remote(
                    ebuf.at[0, j], ebuf.at[1, j], es_sem.at[j - 1], er_sem.at[j - 1],
                    along_y(4 - j),
                )
                for j in (1, 2, 3)
            ]
            for send in coef_sends:
                send.start()
        spread = dot(coef.astype(BF16), stored[...])
        parts = []
        for s in range(SITES):
            at = s * 2 * NB
            parts.append(spread[:, at : at + NB] - turn(spread[:, at + NB : at + 2 * NB]))
        ssend[n] = jnp.concatenate(parts, axis=0).astype(BF16)
        pair = remote(ssend.at[n], srecv.at[n], ss_sem.at[n], sr_sem.at[n], sibling)
        pair.start()
        pair.wait_recv()
        cur[...] = x - (ssend[n].astype(F32) + srecv[n].astype(F32))
        cross.wait_send()
        for send in sends:
            send.wait_send()
        cross_back.wait_send()
        pair.wait_send()

    fbuf[y] = cur[...].astype(BF16)
    final = [
        remote(fbuf.at[y], fbuf.at[y], fs_sem.at[j - 1], fr_sem.at[j - 1], along_y(j))
        for j in (1, 2, 3)
    ]
    for send in final:
        send.start()
    for send in coef_sends:
        send.wait()
    coef_ref[y] = ebuf[0, 0]
    for j in (1, 2, 3):
        coef_ref[ring(j)] = ebuf[1, j]
    for j in (1, 2, 3):
        source = ring(4 - j)
        remote(
            fbuf.at[source], fbuf.at[source], fs_sem.at[j - 1], fr_sem.at[j - 1], along_y(j)
        ).wait_recv()
    for send in final:
        send.wait_send()
    out_ref[...] = fbuf[...]


def shards(start_block, self_block, hop_links, stored_vectors):
    y = lax.rem(lax.axis_index("krylov"), 4)
    mine = lax.dynamic_slice_in_dim(start_block[0], y * QUARTER, QUARTER, axis=1)
    mine = jnp.transpose(mine, (0, 2, 1, 3)).reshape(SITES * ROWS, NB).astype(F32)
    flat = stored_vectors.reshape(GROUP, FLAT)
    vmem, anywhere = pltpu.VMEM, pl.BlockSpec(memory_space=pl.ANY)
    here = pl.BlockSpec(memory_space=vmem)
    dma, block = pltpu.SemaphoreType.DMA, (SITES * ROWS, NB)
    out, coef = pl.pallas_call(
        kernel,
        out_shape=(
            jax.ShapeDtypeStruct((4,) + block, BF16),
            jax.ShapeDtypeStruct((4, ROWS, GROUP), F32),
        ),
        in_specs=[here, anywhere, anywhere, anywhere],
        out_specs=(here, here),
        scratch_shapes=[
            vmem((SITES, 2, NB, NB), BF16),
            vmem((SITES, 2, 2, NB, NB), BF16),
            vmem((SITES, 2, NB, NB), BF16),
            vmem((4 * GROUP, FLAT), BF16),
            vmem(block, F32),
            vmem(block, F32),
            vmem(block, BF16),
            vmem((2,) + block, BF16),
            vmem(block, BF16),
            vmem((2,) + block, BF16),
            vmem((2, ROWS, 2 * GROUP), F32),
            vmem((2, ROWS, 2 * GROUP), F32),
            vmem((2, CHIPS, 2 * ROWS, GROUP), BF16),
            vmem((2, ROWS, 2 * GROUP), F32),
            vmem((2, ROWS, 2 * GROUP), F32),
            vmem((2,) + block, BF16),
            vmem((2,) + block, BF16),
            vmem((4,) + block, BF16),
            vmem((2, 4, ROWS, GROUP), F32),
            dma((3,)),
            dma((2,)), dma((2,)), dma((2,)), dma((2,)),
            dma((3,)), dma((3,)),
            dma((2,)), dma((2,)),
            dma((2, CHIPS)), dma((2, CHIPS)),
            dma((2,)), dma((2,)), dma((2,)), dma((2,)),
            dma((3,)), dma((3,)), dma((3,)), dma((3,)),
        ],
        compiler_params=pltpu.CompilerParams(
            collective_id=0, has_side_effects=True, vmem_limit_bytes=48 * 2**20
        ),
    )(mine, self_block[0], hop_links[0], flat)
    out = out.reshape(4, SITES, 2, QUARTER, NB)
    out = jnp.transpose(out, (1, 0, 3, 2, 4)).reshape(1, SITES, 16, 2, NB)
    coef = coef.reshape(4, 2, QUARTER, GROUP)
    coef = jnp.transpose(coef, (3, 1, 0, 2)).reshape(GROUP, 2, 16)
    return out, coef


def solution(mesh):
    placed = (
        P("lat", None, None, None, None),
        P("lat", None, None, None, None),
        P("lat", None, None, None, None, None),
        P("krylov", "lat", None, None, None),
    )
    return jax.shard_map(
        shards,
        mesh=mesh,
        in_specs=placed,
        out_specs=(P("lat", None, None, None, None), P("krylov", None, None)),
        check_vma=False,
    )
```

time: 577 us -> 95.8 us (0.17)
  the two profiles are of different devices: /device:TPU:32 before, /device:TPU:1 now
where the time goes in v1:
time: 95.8 us; the launch traced here: 95.5 us
  Pallas kernels  89.1 us (93%)
  local copies, waits for them, and re-layouts  4.93 us (5%)
    pallas_call x1, Pallas kernels, shards(): pl.pallas_call(kernel, out_shape=(jax.ShapeDtypeStruct((4,) + block, BF16...  89.1 us
    unnamed x2, local copies, waits for them, and re-layouts  1.92 us

profile of v1, /device:TPU:1, one launch (start us, length us, event | category | flops | bytes accessed | tf_op | source)
XLA Modules:
  0.0 95.5 jit_solution(7468707775486177206)
XLA Ops:
  0.6 0.8 convert_bitcast_fusion
  1.5 1.6 %copy.11.stored_hbm = bf16[128,3200]{1,0:T(8,128)(2,1)S(1)} copy(bf16[128,3200]{0,1:T(8,128)(2,1)} %bitcast.17) | data formatting | bytes 1638400 | tf_op jit(solution)/shard_map/reshape | solution.py:272
  3.1 0.0 copy-start
  3.1 1.9 %copy-done = bf16[1,4,2,400,400]{4,3,2,1,0:T(8,128)(2,1)S(1)} copy-done((bf16[1,4,2,400,400]{4,3,2,1,0:T(8,128)(2,1)S(1)}, bf16[1,4,2,400,400]{4,3,2,1,0:T(8,128)(2,1)}, u32[]{:S(2)}) %copy-start) | copy-done | bytes 2560024
  5.0 89.1 %shard_map.59 = (bf16[4,32,400]{2,1,0:T(8,128)(2,1)S(1)}, f32[4,8,128]{2,1,0:T(8,128)S(1)}) custom-call(f32[32,400]{1,0:T(8,128)S(1)} %reshape.30.start_ref, bf16[4,2,400,400]{3,2,1,0:T(8,128)(2,1)S(1)} %bitcast.14, bf16[4,2,2,400,400]{4,3,2,1,0:T(8,128)(2,1)} %bitcast.16, bf16[128,3200]{1,0:T(8,128)(2,1)S(1)} %copy.11.stored_hbm), custom_call_target="tpu_custom_call" | custom-call | tf_op jit(solution)/shard_map/pallas_call | solution.py:276
  94.2 0.8 copy.12
  94.9 0.6 copy.13
  (3 shorter events, 0.1 us)
Async XLA Ops:
  3.1 1.9 %copy-start = (bf16[1,4,2,400,400]{4,3,2,1,0:T(8,128)(2,1)S(1)}, bf16[1,4,2,400,400]{4,3,2,1,0:T(8,128)(2,1)}, u32[]{:S(2)}) copy-start(bf16[1,4,2,400,400]{4,3,2,1,0:T(8,128)(2,1)} %param.5) | copy-start | bytes 7680004

commit v2 on v1

--- a/solution.py
+++ b/solution.py
@@ -42,8 +42,8 @@
 def kernel(
     start_ref, self_hbm, hop_hbm, stored_hbm,
     out_ref, coef_ref,
-    self_w, hop_w, ahead_w, stored,
-    cur, prev, vsend, vrecv, psend, precv,
+    self_w, space_w, time_w, ahead_w, stored,
+    cur, prev, bsend, vrecv, psend, precv,
     asend, arecv, zbuf, dsend, drecv, ssend, srecv, fbuf, ebuf,
     load_sem, vs_sem, vr_sem, ps_sem, pr_sem, gs_sem, gr_sem,
     as_sem, ar_sem, zs_sem, zr_sem, ds_sem, dr_sem, ss_sem, sr_sem,
@@ -80,57 +80,80 @@
         )
 
     loads = [
-        pltpu.make_async_copy(hop_hbm, hop_w, load_sem.at[0]),
+        pltpu.make_async_copy(hop_hbm.at[:, 1], time_w, load_sem.at[0]),
         pltpu.make_async_copy(self_hbm, self_w, load_sem.at[1]),
-        pltpu.make_async_copy(stored_hbm, stored.at[pl.ds(0, GROUP)], load_sem.at[2]),
+        pltpu.make_async_copy(hop_hbm.at[:, 0], space_w, load_sem.at[2]),
+        pltpu.make_async_copy(stored_hbm, stored.at[:, pl.ds(0, GROUP)], load_sem.at[3]),
     ]
     for load in loads:
         load.start()
     cur[...] = start_ref[...]
     prev[...] = start_ref[...]
+    psend[1] = jnp.zeros_like(psend[1])
     loads[0].wait()
-    row = lax.broadcasted_iota(jnp.int32, (NB, NB), 0)
-    col = lax.broadcasted_iota(jnp.int32, (NB, NB), 1)
-    eye = (row == col).astype(BF16)
-
-    def flip(site, carry):
-        ahead_w[site, 0] = dot_t(eye, hop_w[site, 1, 0]).astype(BF16)
-        ahead_w[site, 1] = (-dot_t(eye, hop_w[site, 1, 1])).astype(BF16)
-        return carry
-
-    lax.fori_loop(0, SITES, flip, 0)
-    loads[1].wait()
 
     pl.semaphore_wait(barrier, len(greet))
 
     gathers = [
         remote(
-            stored_hbm, stored.at[pl.ds(j * GROUP, GROUP)],
+            stored_hbm, stored.at[:, pl.ds(j * GROUP, GROUP)],
             gs_sem.at[j - 1], gr_sem.at[j - 1], along_y(j),
         )
         for j in (1, 2, 3)
     ]
-    for gather in gathers:
-        gather.start()
+
+    def to_behind(slot):
+        return remote(bsend, vrecv.at[slot], vs_sem, vr_sem.at[slot], behind)
+
+    even, odd = core == 0, core == 1
+
+    @pl.when(even)
+    def _():
+        bsend[...] = cur[...].astype(BF16)
+        to_behind(0).start()
+
+    def factor(i):
+        first = lax.rem(i, DEG) == 0
+        return jnp.where(first, 1.0 / HALF_WIDTH, 2.0 / HALF_WIDTH).astype(F32)
 
     def step(i, carry):
-        p = lax.rem(i, 2)
-        first = lax.rem(i, DEG) == 0
-        scale = jnp.where(first, 1.0 / HALF_WIDTH, 2.0 / HALF_WIDTH).astype(F32)
-        keep = jnp.where(first, 0.0, 1.0).astype(F32)
+        p, slot = lax.rem(i, 2), lax.rem(i, 3)
+        scale = factor(i)
+        keep = jnp.where(lax.rem(i, DEG) == 0, 0.0, 1.0).astype(F32)
         x = cur[...]
         xb = x.astype(BF16)
         xt = turn(x).astype(BF16)
-        vsend[...] = xb
-        back = remote(vsend, vrecv.at[p], vs_sem.at[p], vr_sem.at[p], behind)
-        back.start()
+
+        @pl.when(odd)
+        def _():
+            bsend[...] = xb
+            to_behind(slot).start()
+
         parts = []
         for s in range(SITES):
             rows = slice(s * ROWS, s * ROWS + ROWS)
-            parts.append(dot(xb[rows], hop_w[s, 1, 0]) + dot(xt[rows], hop_w[s, 1, 1]))
-        psend[...] = jnp.concatenate(parts, axis=0).astype(BF16)
-        forth = remote(psend, precv.at[p], ps_sem.at[p], pr_sem.at[p], ahead)
+            parts.append(dot(xb[rows], time_w[s, 0]) + dot(xt[rows], time_w[s, 1]))
+        psend[p] = jnp.concatenate(parts, axis=0).astype(BF16)
+        forth = remote(psend.at[p], precv.at[slot], ps_sem, pr_sem.at[slot], ahead)
         forth.start()
+
+        @pl.when(i == 0)
+        def _():
+            for gather in gathers:
+                gather.start()
+            row = lax.broadcasted_iota(jnp.int32, (NB, NB), 0)
+            col = lax.broadcasted_iota(jnp.int32, (NB, NB), 1)
+            eye = (row == col).astype(BF16)
+
+            def flip(site, carry):
+                ahead_w[site, 0] = dot_t(eye, time_w[site, 0]).astype(BF16)
+                ahead_w[site, 1] = (-dot_t(eye, time_w[site, 1])).astype(BF16)
+                return carry
+
+            lax.fori_loop(0, SITES, flip, 0)
+            loads[1].wait()
+            loads[2].wait()
+
         parts = []
         for s in range(SITES):
             rows = slice(s * ROWS, s * ROWS + ROWS)
@@ -139,34 +162,42 @@
             lst = (s - 1) % SITES
             lrows = slice(lst * ROWS, lst * ROWS + ROWS)
             total = dot(xb[rows], self_w[s, 0]) + dot(xt[rows], self_w[s, 1])
-            total += dot(xb[lrows], hop_w[lst, 0, 0]) + dot(xt[lrows], hop_w[lst, 0, 1])
-            total += dot_t(xb[nrows], hop_w[s, 0, 0]) - dot_t(xt[nrows], hop_w[s, 0, 1])
+            total += dot(xb[lrows], space_w[lst, 0]) + dot(xt[lrows], space_w[lst, 1])
+            total += dot_t(xb[nrows], space_w[s, 0]) - dot_t(xt[nrows], space_w[s, 1])
             parts.append(total)
         here = jnp.concatenate(parts, axis=0)
         base = scale * (here - CENTER * x) - keep * prev[...]
-        back.wait_recv()
-        vb = vrecv[p]
-        vt = turn(vb.astype(F32)).astype(BF16)
+        to_behind(slot).wait_recv()
+        known = jnp.where(odd, factor(i + DEG - 1), 0.0) * psend[1 - p].astype(F32)
+        va = vrecv[slot].astype(F32) + known
+        vb, vt = va.astype(BF16), turn(va).astype(BF16)
         parts = []
         for s in range(SITES):
             rows = slice(s * ROWS, s * ROWS + ROWS)
             parts.append(dot(vb[rows], ahead_w[s, 0]) + dot(vt[rows], ahead_w[s, 1]))
-        there = jnp.concatenate(parts, axis=0)
+        base = base + scale * jnp.concatenate(parts, axis=0)
+        to_behind(slot).wait_send()
+
+        @pl.when(jnp.logical_and(even, i < 2 * DEG - 1))
+        def _():
+            bsend[...] = base.astype(BF16)
+            to_behind(lax.rem(i + 1, 3)).start()
+
         forth.wait_recv()
-        there = there + precv[p].astype(F32)
         prev[...] = x
-        cur[...] = base + scale * there
-        back.wait_send()
+        cur[...] = base + scale * precv[slot].astype(F32)
         forth.wait_send()
         return carry
 
     lax.fori_loop(0, 2 * DEG, step, 0)
 
-    loads[2].wait()
+    loads[3].wait()
     for gather in gathers:
         gather.wait()
 
-    total = None
+    my_half = pl.ds(pl.multiple_of(core * 2 * GROUP, 2 * GROUP), 2 * GROUP)
+    its_half = pl.ds(pl.multiple_of((1 - core) * 2 * GROUP, 2 * GROUP), 2 * GROUP)
+    mine_total = other_total = None
     for n in range(2):
         x = cur[...]
         xt = turn(x)
@@ -174,13 +205,29 @@
         for s in range(SITES):
             rows = slice(s * ROWS, s * ROWS + ROWS)
             pieces += [x[rows], xt[rows]]
-        flat = jnp.concatenate(pieces, axis=1).astype(BF16)
-        part = dot_t(flat, stored[...])
-        low, high = part[:, : 2 * GROUP], part[:, 2 * GROUP :]
-        asend[n] = jnp.where(core == 0, high, low)
+        pieces = [piece.astype(BF16) for piece in pieces]
+
+        def project(half):
+            total = None
+            for q, piece in enumerate(pieces):
+                term = dot(piece, stored[q * NB : (q + 1) * NB, half])
+                total = term if total is None else total + term
+            return total
+
+        def spread(coef, half):
+            coef = coef.astype(BF16)
+            parts = []
+            for s in range(SITES):
+                at = s * 2 * NB
+                real = dot_t(coef, stored[at : at + NB, half])
+                imag = dot_t(coef, stored[at + NB : at + 2 * NB, half])
+                parts.append(real - turn(imag))
+            return jnp.concatenate(parts, axis=0)
+
+        asend[n] = project(its_half)
         cross = remote(asend.at[n], arecv.at[n], as_sem.at[n], ar_sem.at[n], partner)
         cross.start()
-        mine = jnp.where(core == 0, low, high)
+        mine = project(my_half)
         cross.wait_recv()
         mine = mine + arecv[n]
         zbuf[n, chip] = jnp.concatenate(
@@ -209,30 +256,27 @@
         dsend[n] = own
         cross_back = remote(dsend.at[n], drecv.at[n], ds_sem.at[n], dr_sem.at[n], partner)
         cross_back.start()
+        change = spread(own, my_half)
         cross_back.wait_recv()
         other = drecv[n]
-        coef = jnp.concatenate(
-            [jnp.where(core == 0, own, other), jnp.where(core == 0, other, own)], axis=1
-        )
-        total = coef if total is None else total + coef
+        mine_total = own if n == 0 else mine_total + own
+        other_total = other if n == 0 else other_total + other
         if n == 1:
-            for j in range(4):
-                ebuf[0, j] = total[:, j * GROUP : (j + 1) * GROUP]
+            low = jnp.where(even, mine_total, other_total)
+            high = jnp.where(even, other_total, mine_total)
+            ebuf[0, 0], ebuf[0, 1] = low[:, :GROUP], low[:, GROUP:]
+            ebuf[0, 2], ebuf[0, 3] = high[:, :GROUP], high[:, GROUP:]
             coef_sends = [
                 remote(
-                    ebuf.at[0, j], ebuf.at[1, j], es_sem.at[j - 1], er_sem.at[j - 1],
+                    ebuf.at[0, j], ebuf.at[1, y], es_sem.at[j - 1], er_sem.at[j - 1],
                     along_y(4 - j),
                 )
                 for j in (1, 2, 3)
             ]
             for send in coef_sends:
                 send.start()
-        spread = dot(coef.astype(BF16), stored[...])
-        parts = []
-        for s in range(SITES):
-            at = s * 2 * NB
-            parts.append(spread[:, at : at + NB] - turn(spread[:, at + NB : at + 2 * NB]))
-        ssend[n] = jnp.concatenate(parts, axis=0).astype(BF16)
+        change = change + spread(other, its_half)
+        ssend[n] = change.astype(BF16)
         pair = remote(ssend.at[n], srecv.at[n], ss_sem.at[n], sr_sem.at[n], sibling)
         pair.start()
         pair.wait_recv()
@@ -250,11 +294,15 @@
     ]
     for send in final:
         send.start()
-    for send in coef_sends:
-        send.wait()
-    coef_ref[y] = ebuf[0, 0]
+    ebuf[1, y] = ebuf[0, 0]
     for j in (1, 2, 3):
-        coef_ref[ring(j)] = ebuf[1, j]
+        source = ring(j)
+        remote(
+            ebuf.at[0, j], ebuf.at[1, source], es_sem.at[j - 1], er_sem.at[j - 1], along_y(4 - j)
+        ).wait()
+    for part in range(2):
+        rows = slice(part * QUARTER, (part + 1) * QUARTER)
+        coef_ref[part] = jnp.concatenate([ebuf[1, q, rows] for q in range(4)], axis=0)
     for j in (1, 2, 3):
         source = ring(4 - j)
         remote(
@@ -269,29 +317,30 @@
     y = lax.rem(lax.axis_index("krylov"), 4)
     mine = lax.dynamic_slice_in_dim(start_block[0], y * QUARTER, QUARTER, axis=1)
     mine = jnp.transpose(mine, (0, 2, 1, 3)).reshape(SITES * ROWS, NB).astype(F32)
-    flat = stored_vectors.reshape(GROUP, FLAT)
-    vmem, anywhere = pltpu.VMEM, pl.BlockSpec(memory_space=pl.ANY)
+    flat = jnp.transpose(stored_vectors.reshape(GROUP, FLAT))
+    vmem, anywhere = pltpu.VMEM, pl.BlockSpec(memory_space=pltpu.HBM)
     here = pl.BlockSpec(memory_space=vmem)
     dma, block = pltpu.SemaphoreType.DMA, (SITES * ROWS, NB)
     out, coef = pl.pallas_call(
         kernel,
         out_shape=(
             jax.ShapeDtypeStruct((4,) + block, BF16),
-            jax.ShapeDtypeStruct((4, ROWS, GROUP), F32),
+            jax.ShapeDtypeStruct((2, 16, GROUP), F32),
         ),
         in_specs=[here, anywhere, anywhere, anywhere],
         out_specs=(here, here),
         scratch_shapes=[
             vmem((SITES, 2, NB, NB), BF16),
-            vmem((SITES, 2, 2, NB, NB), BF16),
             vmem((SITES, 2, NB, NB), BF16),
-            vmem((4 * GROUP, FLAT), BF16),
+            vmem((SITES, 2, NB, NB), BF16),
+            vmem((SITES, 2, NB, NB), BF16),
+            vmem((FLAT, 4 * GROUP), BF16),
             vmem(block, F32),
             vmem(block, F32),
             vmem(block, BF16),
+            vmem((3,) + block, BF16),
             vmem((2,) + block, BF16),
-            vmem(block, BF16),
-            vmem((2,) + block, BF16),
+            vmem((3,) + block, BF16),
             vmem((2, ROWS, 2 * GROUP), F32),
             vmem((2, ROWS, 2 * GROUP), F32),
             vmem((2, CHIPS, 2 * ROWS, GROUP), BF16),
@@ -301,8 +350,8 @@
             vmem((2,) + block, BF16),
             vmem((4,) + block, BF16),
             vmem((2, 4, ROWS, GROUP), F32),
-            dma((3,)),
-            dma((2,)), dma((2,)), dma((2,)), dma((2,)),
+            dma((4,)),
+            dma, dma((3,)), dma, dma((3,)),
             dma((3,)), dma((3,)),
             dma((2,)), dma((2,)),
             dma((2, CHIPS)), dma((2, CHIPS)),
@@ -310,14 +359,12 @@
             dma((3,)), dma((3,)), dma((3,)), dma((3,)),
         ],
         compiler_params=pltpu.CompilerParams(
-            collective_id=0, has_side_effects=True, vmem_limit_bytes=48 * 2**20
+            collective_id=0, has_side_effects=True, vmem_limit_bytes=56 * 2**20
         ),
     )(mine, self_block[0], hop_links[0], flat)
     out = out.reshape(4, SITES, 2, QUARTER, NB)
     out = jnp.transpose(out, (1, 0, 3, 2, 4)).reshape(1, SITES, 16, 2, NB)
-    coef = coef.reshape(4, 2, QUARTER, GROUP)
-    coef = jnp.transpose(coef, (3, 1, 0, 2)).reshape(GROUP, 2, 16)
-    return out, coef
+    return out, jnp.transpose(coef, (2, 0, 1))
 
 
 def solution(mesh):

time: 95.8 us -> 93.6 us (0.977)
  local copies, waits for them, and re-layouts: 4.93 us -> 3.7 us
    reshape x1 -> x0, local copies, waits for them, and re-layouts: 1.56 us -> none  [shards(): flat = stored_vectors.reshape(GROUP, FLAT)]
    pallas_call x1, Pallas kernels: 89.1 us -> 88.2 us  [shards(): pl.pallas_call(kernel, out_shape=(jax.ShapeDtypeStruct((4,) + block, BF16...]
    unnamed x2 -> x1, local copies, waits for them, and re-layouts: 1.92 us -> 1.32 us
where the time goes in v2:
time: 93.6 us; the launch traced here: 93.3 us
  Pallas kernels  88.2 us (94%)
  local copies, waits for them, and re-layouts  3.7 us (4%)
    pallas_call x1, Pallas kernels, shards(): pl.pallas_call(kernel, out_shape=(jax.ShapeDtypeStruct((4,) + block, BF16...  88.2 us

profile of v2, /device:TPU:1, one launch (start us, length us, event | category | flops | bytes accessed | tf_op | source)
XLA Modules:
  0.0 93.3 jit_solution(8010504097445802317)
XLA Ops:
  0.6 0.8 convert_bitcast_fusion
  1.5 0.7 reshape.22.start_ref
  2.1 88.2 %shard_map.59 = (bf16[4,32,400]{2,1,0:T(8,128)(2,1)}, f32[2,16,128]{2,1,0:T(8,128)}) custom-call(f32[32,400]{1,0:T(8,128)} %reshape.22.start_ref, bf16[4,2,400,400]{3,2,1,0:T(8,128)(2,1)} %bitcast.14, bf16[4,2,2,400,400]{4,3,2,1,0:T(8,128)(2,1)} %bitcast.13, bf16[3200,128]{1,0:T(8,128)(2,1)} %bitcast.15), custom_call_target="tpu_custom_call" | custom-call | tf_op jit(solution)/shard_map/pallas_call | solution.py:324
  90.3 0.9 %reshape.20 = bf16[4,4,2,4,400]{4,3,2,1,0:T(4,128)(2,1)S(1)} reshape(bf16[4,32,400]{2,1,0:T(8,128)(2,1)} %get-tuple-element.4) | data formatting | bytes 204800 | tf_op jit(solution)/shard_map/reshape | solution.py:365
  91.2 0.8 copy.7
  92.0 1.3 %copy.9 = f32[128,2,16]{0,2,1:T(8,128)} copy(f32[128,2,16]{0,2,1:T(8,128)} %bitcast.18) | data formatting | bytes 32768
  (1 shorter events, 0.0 us)

commit v3 on v2

--- a/solution.py
+++ b/solution.py
@@ -40,14 +40,14 @@
 
 
 def kernel(
-    start_ref, self_hbm, hop_hbm, stored_hbm,
+    start_hbm, self_hbm, hop_hbm, stored_hbm,
     out_ref, coef_ref,
-    self_w, space_w, time_w, ahead_w, stored,
+    start, self_w, space_w, time_w, ahead_w, stored,
     cur, prev, bsend, vrecv, psend, precv,
     asend, arecv, zbuf, dsend, drecv, ssend, srecv, fbuf, ebuf,
     load_sem, vs_sem, vr_sem, ps_sem, pr_sem, gs_sem, gr_sem,
     as_sem, ar_sem, zs_sem, zr_sem, ds_sem, dr_sem, ss_sem, sr_sem,
-    fs_sem, fr_sem, es_sem, er_sem,
+    fs_sem, fr_sem, es_sem, er_sem, word_sem,
 ):
     lat, kry = lax.axis_index("lat"), lax.axis_index("krylov")
     y, h = lax.rem(kry, 4), kry // 4
@@ -69,7 +69,8 @@
     barrier = pltpu.get_barrier_semaphore()
     greet = [ahead, behind, sibling]
     greet += [along_y(j) for j in (1, 2, 3)]
-    greet += [(other_chip(j) * 2 + core, kry) for j in range(1, CHIPS)]
+    beside_z = [(other_chip(j) * 2 + core, kry) for j in (2, CHIPS - 2)]
+    greet += beside_z
     for device in greet:
         pl.semaphore_signal(barrier, inc=1, device_id=device, device_id_type=MESH)
 
@@ -84,14 +85,29 @@
         pltpu.make_async_copy(self_hbm, self_w, load_sem.at[1]),
         pltpu.make_async_copy(hop_hbm.at[:, 0], space_w, load_sem.at[2]),
         pltpu.make_async_copy(stored_hbm, stored.at[:, pl.ds(0, GROUP)], load_sem.at[3]),
+        pltpu.make_async_copy(
+            start_hbm.at[:, pl.ds(y * QUARTER, QUARTER)], start, load_sem.at[4]
+        ),
     ]
-    for load in loads:
-        load.start()
-    cur[...] = start_ref[...]
-    prev[...] = start_ref[...]
+    for q in (4, 0, 1, 2, 3):
+        loads[q].start()
+    loads[4].wait()
+    block = start[...].astype(F32)
+    block = jnp.concatenate(
+        [block[s, r, c : c + 1] for s in range(SITES) for c in range(2) for r in range(QUARTER)],
+        axis=0,
+    )
+    cur[...] = block
+    prev[...] = block
     psend[1] = jnp.zeros_like(psend[1])
     loads[0].wait()
 
+    def flip(site, carry):
+        ahead_w[site, 0] = jnp.transpose(time_w[site, 0])
+        ahead_w[site, 1] = -jnp.transpose(time_w[site, 1])
+        return carry
+
+    lax.fori_loop(0, SITES, flip, 0)
     pl.semaphore_wait(barrier, len(greet))
 
     gathers = [
@@ -116,6 +132,20 @@
         first = lax.rem(i, DEG) == 0
         return jnp.where(first, 1.0 / HALF_WIDTH, 2.0 / HALF_WIDTH).astype(F32)
 
+    def meet(i):
+        for turn_at in range(5):
+
+            @pl.when(i == 2 * turn_at + 2)
+            def _():
+                if turn_at > 0:
+                    pl.semaphore_wait(word_sem.at[turn_at - 1, 0], 1)
+                    pl.semaphore_wait(word_sem.at[turn_at - 1, 1], 1)
+                if turn_at < 4:
+                    for q, device in enumerate(beside_z):
+                        pl.semaphore_signal(
+                            word_sem.at[turn_at, q], inc=1, device_id=device, device_id_type=MESH
+                        )
+
     def step(i, carry):
         p, slot = lax.rem(i, 2), lax.rem(i, 3)
         scale = factor(i)
@@ -136,21 +166,12 @@
         psend[p] = jnp.concatenate(parts, axis=0).astype(BF16)
         forth = remote(psend.at[p], precv.at[slot], ps_sem, pr_sem.at[slot], ahead)
         forth.start()
+        meet(i)
 
         @pl.when(i == 0)
         def _():
             for gather in gathers:
                 gather.start()
-            row = lax.broadcasted_iota(jnp.int32, (NB, NB), 0)
-            col = lax.broadcasted_iota(jnp.int32, (NB, NB), 1)
-            eye = (row == col).astype(BF16)
-
-            def flip(site, carry):
-                ahead_w[site, 0] = dot_t(eye, time_w[site, 0]).astype(BF16)
-                ahead_w[site, 1] = (-dot_t(eye, time_w[site, 1])).astype(BF16)
-                return carry
-
-            lax.fori_loop(0, SITES, flip, 0)
             loads[1].wait()
             loads[2].wait()
 
@@ -314,9 +335,6 @@
 
 
 def shards(start_block, self_block, hop_links, stored_vectors):
-    y = lax.rem(lax.axis_index("krylov"), 4)
-    mine = lax.dynamic_slice_in_dim(start_block[0], y * QUARTER, QUARTER, axis=1)
-    mine = jnp.transpose(mine, (0, 2, 1, 3)).reshape(SITES * ROWS, NB).astype(F32)
     flat = jnp.transpose(stored_vectors.reshape(GROUP, FLAT))
     vmem, anywhere = pltpu.VMEM, pl.BlockSpec(memory_space=pltpu.HBM)
     here = pl.BlockSpec(memory_space=vmem)
@@ -327,9 +345,10 @@
             jax.ShapeDtypeStruct((4,) + block, BF16),
             jax.ShapeDtypeStruct((2, 16, GROUP), F32),
         ),
-        in_specs=[here, anywhere, anywhere, anywhere],
+        in_specs=[anywhere] * 4,
         out_specs=(here, here),
         scratch_shapes=[
+            vmem((SITES, QUARTER, 2, NB), BF16),
             vmem((SITES, 2, NB, NB), BF16),
             vmem((SITES, 2, NB, NB), BF16),
             vmem((SITES, 2, NB, NB), BF16),
@@ -350,18 +369,19 @@
             vmem((2,) + block, BF16),
             vmem((4,) + block, BF16),
             vmem((2, 4, ROWS, GROUP), F32),
-            dma((4,)),
+            dma((5,)),
             dma, dma((3,)), dma, dma((3,)),
             dma((3,)), dma((3,)),
             dma((2,)), dma((2,)),
             dma((2, CHIPS)), dma((2, CHIPS)),
             dma((2,)), dma((2,)), dma((2,)), dma((2,)),
             dma((3,)), dma((3,)), dma((3,)), dma((3,)),
+            pltpu.SemaphoreType.REGULAR((4, 2)),
         ],
         compiler_params=pltpu.CompilerParams(
-            collective_id=0, has_side_effects=True, vmem_limit_bytes=56 * 2**20
+            collective_id=0, has_side_effects=True, vmem_limit_bytes=55000 * 2**10
         ),
-    )(mine, self_block[0], hop_links[0], flat)
+    )(start_block[0], self_block[0], hop_links[0], flat)
     out = out.reshape(4, SITES, 2, QUARTER, NB)
     out = jnp.transpose(out, (1, 0, 3, 2, 4)).reshape(1, SITES, 16, 2, NB)
     return out, jnp.transpose(coef, (2, 0, 1))

time: 93.6 us -> 85.1 us (0.909)
  Pallas kernels: 88.2 us -> 83 us
  local copies, waits for them, and re-layouts: 3.7 us -> 1.4 us
    pallas_call x1, Pallas kernels: 88.2 us -> 83 us  [shards(): pl.pallas_call(kernel, out_shape=(jax.ShapeDtypeStruct((4,) + block, BF16...]
where the time goes in v3:
time: 85.1 us; the launch traced here: 85 us
  Pallas kernels  83 us (98%)
  local copies, waits for them, and re-layouts  1.4 us (2%)
    pallas_call x1, Pallas kernels, shards(): pl.pallas_call(kernel, out_shape=(jax.ShapeDtypeStruct((4,) + block, BF16...  83 us

profile of v3, /device:TPU:1, one launch (start us, length us, event | category | flops | bytes accessed | tf_op | source)
XLA Modules:
  0.0 85.0 jit_solution(3776550431944954088)
XLA Ops:
  0.6 83.0 %shard_map.59 = (bf16[4,32,400]{2,1,0:T(8,128)(2,1)S(1)}, f32[2,16,128]{2,1,0:T(8,128)S(1)}) custom-call(bf16[4,16,2,400]{3,2,1,0:T(2,128)(2,1)} %bitcast.14, bf16[4,2,400,400]{3,2,1,0:T(8,128)(2,1)} %bitcast.11, bf16[4,2,2,400,400]{4,3,2,1,0:T(8,128)(2,1)} %bitcast.10, bf16[3200,128]{1,0:T(8,128)(2,1)} %bitcast.12), custom_call_target="tpu_custom_call" | custom-call | tf_op jit(solution)/shard_map/pallas_call | solution.py:342
  83.7 0.8 copy.6
  84.4 0.6 copy.8
  (1 shorter events, 0.0 us)

commit v4 on v3

--- a/solution.py
+++ b/solution.py
@@ -42,8 +42,8 @@
 def kernel(
     start_hbm, self_hbm, hop_hbm, stored_hbm,
     out_ref, coef_ref,
-    start, self_w, space_w, time_w, ahead_w, stored,
-    cur, prev, bsend, vrecv, psend, precv,
+    start, self_w, space_w, time_w, ahead_w, beside_w, stored,
+    cur, prev, acc, base, bsend, vrecv, psend, precv,
     asend, arecv, zbuf, dsend, drecv, ssend, srecv, fbuf, ebuf,
     load_sem, vs_sem, vr_sem, ps_sem, pr_sem, gs_sem, gr_sem,
     as_sem, ar_sem, zs_sem, zr_sem, ds_sem, dr_sem, ss_sem, sr_sem,
@@ -102,12 +102,20 @@
     psend[1] = jnp.zeros_like(psend[1])
     loads[0].wait()
 
-    def flip(site, carry):
+    def flip_time(site, carry):
         ahead_w[site, 0] = jnp.transpose(time_w[site, 0])
         ahead_w[site, 1] = -jnp.transpose(time_w[site, 1])
         return carry
 
-    lax.fori_loop(0, SITES, flip, 0)
+    def flip_space(site, carry):
+        beside_w[site, 0] = jnp.transpose(space_w[site, 0])
+        beside_w[site, 1] = -jnp.transpose(space_w[site, 1])
+        return carry
+
+    lax.fori_loop(0, SITES, flip_time, 0)
+    loads[1].wait()
+    loads[2].wait()
+    lax.fori_loop(0, SITES, flip_space, 0)
     pl.semaphore_wait(barrier, len(greet))
 
     gathers = [
@@ -118,15 +126,20 @@
         for j in (1, 2, 3)
     ]
 
-    def to_behind(slot):
-        return remote(bsend, vrecv.at[slot], vs_sem, vr_sem.at[slot], behind)
-
     even, odd = core == 0, core == 1
-
-    @pl.when(even)
-    def _():
-        bsend[...] = cur[...].astype(BF16)
-        to_behind(0).start()
+    halves = (pl.ds(0, 2 * ROWS), pl.ds(2 * ROWS, 2 * ROWS))
+
+    def to_behind(slot, half):
+        return remote(
+            bsend.at[halves[half]], vrecv.at[slot, halves[half]],
+            vs_sem.at[half], vr_sem.at[slot, half], behind,
+        )
+
+    def to_ahead(parity, slot, half):
+        return remote(
+            psend.at[parity, halves[half]], precv.at[slot, halves[half]],
+            ps_sem.at[parity, half], pr_sem.at[slot, half], ahead,
+        )
 
     def factor(i):
         first = lax.rem(i, DEG) == 0
@@ -146,71 +159,142 @@
                             word_sem.at[turn_at, q], inc=1, device_id=device, device_id_type=MESH
                         )
 
+    last = 2 * DEG - 1
+
+    def split(half):
+        x = cur[halves[half]]
+        return [
+            (q.astype(BF16), turn(q).astype(BF16)) for q in (x[:ROWS], x[ROWS:])
+        ]
+
+    def apply(pair, weight, site):
+        return dot(pair[0], weight[site, 0]) + dot(pair[1], weight[site, 1])
+
+    def product(half, i):
+        pairs = split(half)
+        psend[lax.rem(i, 2), halves[half]] = jnp.concatenate(
+            [apply(pairs[q], time_w, 2 * half + q) for q in range(2)], axis=0
+        ).astype(BF16)
+        to_ahead(lax.rem(i, 2), lax.rem(i, 3), half).start()
+
+    def put(site, value, add=True):
+        at = pl.ds(site * ROWS, ROWS)
+        acc[at] = acc[at] + value if add else value
+
+    def from_first():
+        zero, one = split(0)
+        put(0, apply(zero, self_w, 0) + apply(one, beside_w, 0), False)
+        put(1, apply(one, self_w, 1) + apply(zero, space_w, 0), False)
+        put(2, apply(one, space_w, 1), False)
+        put(3, apply(zero, beside_w, 3), False)
+
+    def second_to_first():
+        two, three = split(1)
+        put(0, apply(three, space_w, 3))
+        put(1, apply(two, beside_w, 1))
+
+    def second_to_second():
+        two, three = split(1)
+        put(2, apply(two, self_w, 2) + apply(three, beside_w, 2))
+        put(3, apply(three, self_w, 3) + apply(two, space_w, 2))
+
+    def own_terms(half, i):
+        at = halves[half]
+        keep = jnp.where(lax.rem(i, DEG) == 0, 0.0, 1.0).astype(F32)
+        return factor(i) * (acc[at] - CENTER * cur[at]) - keep * prev[at]
+
+    def from_ahead(half, i, known):
+        to_behind(lax.rem(i, 3), half).wait_recv()
+        v = vrecv[lax.rem(i, 3), halves[half]].astype(F32)
+        if known:
+            earlier = lax.rem(i + 1, 2)
+            v = v + factor(i + DEG - 1) * psend[earlier, halves[half]].astype(F32)
+        pairs = [(q.astype(BF16), turn(q).astype(BF16)) for q in (v[:ROWS], v[ROWS:])]
+        return factor(i) * jnp.concatenate(
+            [apply(pairs[q], ahead_w, 2 * half + q) for q in range(2)], axis=0
+        )
+
+    def finish(half, i, value):
+        at = halves[half]
+        to_ahead(0, lax.rem(i, 3), half).wait_recv()
+        value = value + factor(i) * precv[lax.rem(i, 3), at].astype(F32)
+        prev[at] = cur[at]
+        cur[at] = value
+
+    def send_behind(half, slot, value):
+        to_behind(slot, half).wait_send()
+        bsend[halves[half]] = value.astype(BF16)
+        to_behind(slot, half).start()
+
+    def next_product(half, i):
+        @pl.when(i >= 1)
+        def _():
+            to_ahead(lax.rem(i + 1, 2), 0, half).wait_send()
+
+        product(half, i + 1)
+
+    def even_step(i):
+        second_to_first()
+        base[halves[0]] = own_terms(0, i) + from_ahead(0, i, False)
+
+        @pl.when(i < last)
+        def _():
+            send_behind(0, lax.rem(i + 1, 3), base[halves[0]])
+
+        second_to_second()
+        base[halves[1]] = own_terms(1, i) + from_ahead(1, i, False)
+
+        @pl.when(i < last)
+        def _():
+            send_behind(1, lax.rem(i + 1, 3), base[halves[1]])
+
+        finish(0, i, base[halves[0]])
+
+        @pl.when(i < last)
+        def _():
+            next_product(0, i)
+            from_first()
+
+        finish(1, i, base[halves[1]])
+
+        @pl.when(i < last)
+        def _():
+            next_product(1, i)
+
+    def odd_step(i):
+        from_first()
+        second_to_first()
+        second_to_second()
+        for half in range(2):
+            finish(half, i, own_terms(half, i) + from_ahead(half, i, True))
+
+            @pl.when(i < last)
+            def _(half=half):
+                send_behind(half, lax.rem(i + 1, 3), cur[halves[half]])
+                next_product(half, i)
+
+    bsend[...] = cur[...].astype(BF16)
+    for half in range(2):
+        to_behind(0, half).start()
+        product(half, 0)
+    for gather in gathers:
+        gather.start()
+
+    @pl.when(even)
+    def _():
+        from_first()
+
     def step(i, carry):
-        p, slot = lax.rem(i, 2), lax.rem(i, 3)
-        scale = factor(i)
-        keep = jnp.where(lax.rem(i, DEG) == 0, 0.0, 1.0).astype(F32)
-        x = cur[...]
-        xb = x.astype(BF16)
-        xt = turn(x).astype(BF16)
-
-        @pl.when(odd)
-        def _():
-            bsend[...] = xb
-            to_behind(slot).start()
-
-        parts = []
-        for s in range(SITES):
-            rows = slice(s * ROWS, s * ROWS + ROWS)
-            parts.append(dot(xb[rows], time_w[s, 0]) + dot(xt[rows], time_w[s, 1]))
-        psend[p] = jnp.concatenate(parts, axis=0).astype(BF16)
-        forth = remote(psend.at[p], precv.at[slot], ps_sem, pr_sem.at[slot], ahead)
-        forth.start()
         meet(i)
-
-        @pl.when(i == 0)
-        def _():
-            for gather in gathers:
-                gather.start()
-            loads[1].wait()
-            loads[2].wait()
-
-        parts = []
-        for s in range(SITES):
-            rows = slice(s * ROWS, s * ROWS + ROWS)
-            nxt = (s + 1) % SITES
-            nrows = slice(nxt * ROWS, nxt * ROWS + ROWS)
-            lst = (s - 1) % SITES
-            lrows = slice(lst * ROWS, lst * ROWS + ROWS)
-            total = dot(xb[rows], self_w[s, 0]) + dot(xt[rows], self_w[s, 1])
-            total += dot(xb[lrows], space_w[lst, 0]) + dot(xt[lrows], space_w[lst, 1])
-            total += dot_t(xb[nrows], space_w[s, 0]) - dot_t(xt[nrows], space_w[s, 1])
-            parts.append(total)
-        here = jnp.concatenate(parts, axis=0)
-        base = scale * (here - CENTER * x) - keep * prev[...]
-        to_behind(slot).wait_recv()
-        known = jnp.where(odd, factor(i + DEG - 1), 0.0) * psend[1 - p].astype(F32)
-        va = vrecv[slot].astype(F32) + known
-        vb, vt = va.astype(BF16), turn(va).astype(BF16)
-        parts = []
-        for s in range(SITES):
-            rows = slice(s * ROWS, s * ROWS + ROWS)
-            parts.append(dot(vb[rows], ahead_w[s, 0]) + dot(vt[rows], ahead_w[s, 1]))
-        base = base + scale * jnp.concatenate(parts, axis=0)
-        to_behind(slot).wait_send()
-
-        @pl.when(jnp.logical_and(even, i < 2 * DEG - 1))
-        def _():
-            bsend[...] = base.astype(BF16)
-            to_behind(lax.rem(i + 1, 3)).start()
-
-        forth.wait_recv()
-        prev[...] = x
-        cur[...] = base + scale * precv[slot].astype(F32)
-        forth.wait_send()
+        pl.when(even)(lambda: even_step(i))
+        pl.when(odd)(lambda: odd_step(i))
         return carry
 
     lax.fori_loop(0, 2 * DEG, step, 0)
+    for half in range(2):
+        to_behind(0, half).wait_send()
+        to_ahead(0, 0, half).wait_send()
+        to_ahead(1, 0, half).wait_send()
 
     loads[3].wait()
     for gather in gathers:
@@ -353,7 +437,10 @@
             vmem((SITES, 2, NB, NB), BF16),
             vmem((SITES, 2, NB, NB), BF16),
             vmem((SITES, 2, NB, NB), BF16),
+            vmem((SITES, 2, NB, NB), BF16),
             vmem((FLAT, 4 * GROUP), BF16),
+            vmem(block, F32),
+            vmem(block, F32),
             vmem(block, F32),
             vmem(block, F32),
             vmem(block, BF16),
@@ -370,7 +457,7 @@
             vmem((4,) + block, BF16),
             vmem((2, 4, ROWS, GROUP), F32),
             dma((5,)),
-            dma, dma((3,)), dma, dma((3,)),
+            dma((2,)), dma((3, 2)), dma((2, 2)), dma((3, 2)),
             dma((3,)), dma((3,)),
             dma((2,)), dma((2,)),
             dma((2, CHIPS)), dma((2, CHIPS)),

time: 85.1 us -> 81.6 us (0.959)
  Pallas kernels: 83 us -> 79.5 us
    pallas_call x1, Pallas kernels: 83 us -> 79.5 us  [shards(): pl.pallas_call(kernel, out_shape=(jax.ShapeDtypeStruct((4,) + block, BF16...]
where the time goes in v4:
time: 81.6 us; the launch traced here: 81.5 us
  Pallas kernels  79.5 us (97%)
  local copies, waits for them, and re-layouts  1.4 us (2%)
    pallas_call x1, Pallas kernels, shards(): pl.pallas_call(kernel, out_shape=(jax.ShapeDtypeStruct((4,) + block, BF16...  79.5 us

profile of v4, /device:TPU:1, one launch (start us, length us, event | category | flops | bytes accessed | tf_op | source)
XLA Modules:
  0.0 81.5 jit_solution(996439419269134076)
XLA Ops:
  0.6 79.5 %shard_map.59 = (bf16[4,32,400]{2,1,0:T(8,128)(2,1)S(1)}, f32[2,16,128]{2,1,0:T(8,128)S(1)}) custom-call(bf16[4,16,2,400]{3,2,1,0:T(2,128)(2,1)} %bitcast.14, bf16[4,2,400,400]{3,2,1,0:T(8,128)(2,1)} %bitcast.11, bf16[4,2,2,400,400]{4,3,2,1,0:T(8,128)(2,1)} %bitcast.10, bf16[3200,128]{1,0:T(8,128)(2,1)} %bitcast.12), custom_call_target="tpu_custom_call" | custom-call | tf_op jit(solution)/shard_map/pallas_call | solution.py:426
  80.2 0.8 copy.6
  80.9 0.6 copy.8
  (1 shorter events, 0.0 us)

commit v5 on v4

--- a/solution.py
+++ b/solution.py
@@ -42,7 +42,7 @@
 def kernel(
     start_hbm, self_hbm, hop_hbm, stored_hbm,
     out_ref, coef_ref,
-    start, self_w, space_w, time_w, ahead_w, beside_w, stored,
+    start, self_w, space_w, time_w, ahead_w, stored,
     cur, prev, acc, base, bsend, vrecv, psend, precv,
     asend, arecv, zbuf, dsend, drecv, ssend, srecv, fbuf, ebuf,
     load_sem, vs_sem, vr_sem, ps_sem, pr_sem, gs_sem, gr_sem,
@@ -79,6 +79,27 @@
             src_ref=src, dst_ref=dst, send_sem=send_sem, recv_sem=recv_sem,
             device_id=device, device_id_type=MESH,
         )
+
+    even, odd = core == 0, core == 1
+    halves = (pl.ds(0, 2 * ROWS), pl.ds(2 * ROWS, 2 * ROWS))
+
+    def split(half):
+        x = cur[halves[half]]
+        return [
+            (q.astype(BF16), turn(q).astype(BF16)) for q in (x[:ROWS], x[ROWS:])
+        ]
+
+    def apply(pair, weight, site):
+        return dot(pair[0], weight[site, 0]) + dot(pair[1], weight[site, 1])
+
+    def product(half, i):
+        pairs = split(half)
+        psend[lax.rem(i, 2), halves[half]] = jnp.concatenate(
+            [apply(pairs[q], time_w, 2 * half + q) for q in range(2)], axis=0
+        ).astype(BF16)
+
+    def apply_forward(pair, weight, site):
+        return dot_t(pair[0], weight[site, 0]) - dot_t(pair[1], weight[site, 1])
 
     loads = [
         pltpu.make_async_copy(hop_hbm.at[:, 1], time_w, load_sem.at[0]),
@@ -102,20 +123,11 @@
     psend[1] = jnp.zeros_like(psend[1])
     loads[0].wait()
 
-    def flip_time(site, carry):
+    for half in range(2):
+        product(half, 0)
+    for site in range(SITES):
         ahead_w[site, 0] = jnp.transpose(time_w[site, 0])
         ahead_w[site, 1] = -jnp.transpose(time_w[site, 1])
-        return carry
-
-    def flip_space(site, carry):
-        beside_w[site, 0] = jnp.transpose(space_w[site, 0])
-        beside_w[site, 1] = -jnp.transpose(space_w[site, 1])
-        return carry
-
-    lax.fori_loop(0, SITES, flip_time, 0)
-    loads[1].wait()
-    loads[2].wait()
-    lax.fori_loop(0, SITES, flip_space, 0)
     pl.semaphore_wait(barrier, len(greet))
 
     gathers = [
@@ -125,9 +137,6 @@
         )
         for j in (1, 2, 3)
     ]
-
-    even, odd = core == 0, core == 1
-    halves = (pl.ds(0, 2 * ROWS), pl.ds(2 * ROWS, 2 * ROWS))
 
     def to_behind(slot, half):
         return remote(
@@ -161,41 +170,25 @@
 
     last = 2 * DEG - 1
 
-    def split(half):
-        x = cur[halves[half]]
-        return [
-            (q.astype(BF16), turn(q).astype(BF16)) for q in (x[:ROWS], x[ROWS:])
-        ]
-
-    def apply(pair, weight, site):
-        return dot(pair[0], weight[site, 0]) + dot(pair[1], weight[site, 1])
-
-    def product(half, i):
-        pairs = split(half)
-        psend[lax.rem(i, 2), halves[half]] = jnp.concatenate(
-            [apply(pairs[q], time_w, 2 * half + q) for q in range(2)], axis=0
-        ).astype(BF16)
-        to_ahead(lax.rem(i, 2), lax.rem(i, 3), half).start()
-
     def put(site, value, add=True):
         at = pl.ds(site * ROWS, ROWS)
         acc[at] = acc[at] + value if add else value
 
     def from_first():
         zero, one = split(0)
-        put(0, apply(zero, self_w, 0) + apply(one, beside_w, 0), False)
+        put(0, apply(zero, self_w, 0) + apply_forward(one, space_w, 0), False)
         put(1, apply(one, self_w, 1) + apply(zero, space_w, 0), False)
         put(2, apply(one, space_w, 1), False)
-        put(3, apply(zero, beside_w, 3), False)
+        put(3, apply_forward(zero, space_w, 3), False)
 
     def second_to_first():
         two, three = split(1)
         put(0, apply(three, space_w, 3))
-        put(1, apply(two, beside_w, 1))
+        put(1, apply_forward(two, space_w, 1))
 
     def second_to_second():
         two, three = split(1)
-        put(2, apply(two, self_w, 2) + apply(three, beside_w, 2))
+        put(2, apply(two, self_w, 2) + apply_forward(three, space_w, 2))
         put(3, apply(three, self_w, 3) + apply(two, space_w, 2))
 
     def own_terms(half, i):
@@ -232,6 +225,7 @@
             to_ahead(lax.rem(i + 1, 2), 0, half).wait_send()
 
         product(half, i + 1)
+        to_ahead(lax.rem(i + 1, 2), lax.rem(i + 1, 3), half).start()
 
     def even_step(i):
         second_to_first()
@@ -276,9 +270,11 @@
     bsend[...] = cur[...].astype(BF16)
     for half in range(2):
         to_behind(0, half).start()
-        product(half, 0)
+        to_ahead(0, 0, half).start()
     for gather in gathers:
         gather.start()
+    loads[1].wait()
+    loads[2].wait()
 
     @pl.when(even)
     def _():
@@ -437,7 +433,6 @@
             vmem((SITES, 2, NB, NB), BF16),
             vmem((SITES, 2, NB, NB), BF16),
             vmem((SITES, 2, NB, NB), BF16),
-            vmem((SITES, 2, NB, NB), BF16),
             vmem((FLAT, 4 * GROUP), BF16),
             vmem(block, F32),
             vmem(block, F32),

time: 81.6 us -> 81.7 us (level)
  no operation moved by 1% of the time
where the time goes in v5:
time: 81.7 us; the launch traced here: 81.6 us
  Pallas kernels  79.5 us (97%)
  local copies, waits for them, and re-layouts  1.4 us (2%)
    pallas_call x1, Pallas kernels, shards(): pl.pallas_call(kernel, out_shape=(jax.ShapeDtypeStruct((4,) + block, BF16...  79.5 us

profile of v5, /device:TPU:1, one launch (start us, length us, event | category | flops | bytes accessed | tf_op | source)
XLA Modules:
  0.0 81.6 jit_solution(17284313667961450550)
XLA Ops:
  0.6 79.5 %shard_map.59 = (bf16[4,32,400]{2,1,0:T(8,128)(2,1)S(1)}, f32[2,16,128]{2,1,0:T(8,128)S(1)}) custom-call(bf16[4,16,2,400]{3,2,1,0:T(2,128)(2,1)} %bitcast.14, bf16[4,2,400,400]{3,2,1,0:T(8,128)(2,1)} %bitcast.11, bf16[4,2,2,400,400]{4,3,2,1,0:T(8,128)(2,1)} %bitcast.10, bf16[3200,128]{1,0:T(8,128)(2,1)} %bitcast.12), custom_call_target="tpu_custom_call" | custom-call | tf_op jit(solution)/shard_map/pallas_call | solution.py:422
  80.2 0.8 copy.6
  81.0 0.6 copy.8
  (1 shorter events, 0.0 us)

commit v6 on v5

--- a/solution.py
+++ b/solution.py
@@ -42,7 +42,7 @@
 def kernel(
     start_hbm, self_hbm, hop_hbm, stored_hbm,
     out_ref, coef_ref,
-    start, self_w, space_w, time_w, ahead_w, stored,
+    start, self_w, space_w, time_w, ahead_w, beside_w, stored,
     cur, prev, acc, base, bsend, vrecv, psend, precv,
     asend, arecv, zbuf, dsend, drecv, ssend, srecv, fbuf, ebuf,
     load_sem, vs_sem, vr_sem, ps_sem, pr_sem, gs_sem, gr_sem,
@@ -98,9 +98,6 @@
             [apply(pairs[q], time_w, 2 * half + q) for q in range(2)], axis=0
         ).astype(BF16)
 
-    def apply_forward(pair, weight, site):
-        return dot_t(pair[0], weight[site, 0]) - dot_t(pair[1], weight[site, 1])
-
     loads = [
         pltpu.make_async_copy(hop_hbm.at[:, 1], time_w, load_sem.at[0]),
         pltpu.make_async_copy(self_hbm, self_w, load_sem.at[1]),
@@ -110,7 +107,7 @@
             start_hbm.at[:, pl.ds(y * QUARTER, QUARTER)], start, load_sem.at[4]
         ),
     ]
-    for q in (4, 0, 1, 2, 3):
+    for q in (4, 0, 2, 1, 3):
         loads[q].start()
     loads[4].wait()
     block = start[...].astype(F32)
@@ -125,9 +122,26 @@
 
     for half in range(2):
         product(half, 0)
-    for site in range(SITES):
-        ahead_w[site, 0] = jnp.transpose(time_w[site, 0])
-        ahead_w[site, 1] = -jnp.transpose(time_w[site, 1])
+
+    def unit(n):
+        row = lax.broadcasted_iota(jnp.int32, (n, n), 0)
+        return (row == lax.broadcasted_iota(jnp.int32, (n, n), 1)).astype(BF16)
+
+    def flip(weight, flipped, by_product):
+        for site in range(SITES):
+            for part in range(2):
+                source = weight[site, part]
+                if (site, part) in by_product:
+                    value = jnp.concatenate(
+                        [dot_t(unit(256), source[:, :256]), dot_t(unit(144), source[:, 256:])], axis=0
+                    ).astype(BF16)
+                else:
+                    value = jnp.transpose(source)
+                flipped[site, part] = -value if part else value
+
+    flip(time_w, ahead_w, ((1, 0), (3, 0)))
+    loads[2].wait()
+    flip(space_w, beside_w, ((0, 1), (1, 1), (2, 1)))
     pl.semaphore_wait(barrier, len(greet))
 
     gathers = [
@@ -176,19 +190,19 @@
 
     def from_first():
         zero, one = split(0)
-        put(0, apply(zero, self_w, 0) + apply_forward(one, space_w, 0), False)
+        put(0, apply(zero, self_w, 0) + apply(one, beside_w, 0), False)
         put(1, apply(one, self_w, 1) + apply(zero, space_w, 0), False)
         put(2, apply(one, space_w, 1), False)
-        put(3, apply_forward(zero, space_w, 3), False)
+        put(3, apply(zero, beside_w, 3), False)
 
     def second_to_first():
         two, three = split(1)
         put(0, apply(three, space_w, 3))
-        put(1, apply_forward(two, space_w, 1))
+        put(1, apply(two, beside_w, 1))
 
     def second_to_second():
         two, three = split(1)
-        put(2, apply(two, self_w, 2) + apply_forward(three, space_w, 2))
+        put(2, apply(two, self_w, 2) + apply(three, beside_w, 2))
         put(3, apply(three, self_w, 3) + apply(two, space_w, 2))
 
     def own_terms(half, i):
@@ -274,7 +288,6 @@
     for gather in gathers:
         gather.start()
     loads[1].wait()
-    loads[2].wait()
 
     @pl.when(even)
     def _():
@@ -299,36 +312,33 @@
     my_half = pl.ds(pl.multiple_of(core * 2 * GROUP, 2 * GROUP), 2 * GROUP)
     its_half = pl.ds(pl.multiple_of((1 - core) * 2 * GROUP, 2 * GROUP), 2 * GROUP)
     mine_total = other_total = None
+
+    def project(half, columns):
+        total = None
+        for q, pair in enumerate(split(half)):
+            for part in range(2):
+                at = ((2 * half + q) * 2 + part) * NB
+                term = dot(pair[part], stored[at : at + NB, columns])
+                total = term if total is None else total + term
+        return total
+
+    def spread(coef, half, columns):
+        coef = coef.astype(BF16)
+        parts = []
+        for site in (2 * half, 2 * half + 1):
+            at = site * 2 * NB
+            real = dot_t(coef, stored[at : at + NB, columns])
+            imag = dot_t(coef, stored[at + NB : at + 2 * NB, columns])
+            parts.append(real - turn(imag))
+        return jnp.concatenate(parts, axis=0)
+
+    final = []
+    theirs = project(0, its_half) + project(1, its_half)
     for n in range(2):
-        x = cur[...]
-        xt = turn(x)
-        pieces = []
-        for s in range(SITES):
-            rows = slice(s * ROWS, s * ROWS + ROWS)
-            pieces += [x[rows], xt[rows]]
-        pieces = [piece.astype(BF16) for piece in pieces]
-
-        def project(half):
-            total = None
-            for q, piece in enumerate(pieces):
-                term = dot(piece, stored[q * NB : (q + 1) * NB, half])
-                total = term if total is None else total + term
-            return total
-
-        def spread(coef, half):
-            coef = coef.astype(BF16)
-            parts = []
-            for s in range(SITES):
-                at = s * 2 * NB
-                real = dot_t(coef, stored[at : at + NB, half])
-                imag = dot_t(coef, stored[at + NB : at + 2 * NB, half])
-                parts.append(real - turn(imag))
-            return jnp.concatenate(parts, axis=0)
-
-        asend[n] = project(its_half)
+        asend[n] = theirs
         cross = remote(asend.at[n], arecv.at[n], as_sem.at[n], ar_sem.at[n], partner)
         cross.start()
-        mine = project(my_half)
+        mine = project(0, my_half) + project(1, my_half)
         cross.wait_recv()
         mine = mine + arecv[n]
         zbuf[n, chip] = jnp.concatenate(
@@ -357,7 +367,7 @@
         dsend[n] = own
         cross_back = remote(dsend.at[n], drecv.at[n], ds_sem.at[n], dr_sem.at[n], partner)
         cross_back.start()
-        change = spread(own, my_half)
+        change = [spread(own, half, my_half) for half in range(2)]
         cross_back.wait_recv()
         other = drecv[n]
         mine_total = own if n == 0 else mine_total + own
@@ -376,25 +386,38 @@
             ]
             for send in coef_sends:
                 send.start()
-        change = change + spread(other, its_half)
-        ssend[n] = change.astype(BF16)
-        pair = remote(ssend.at[n], srecv.at[n], ss_sem.at[n], sr_sem.at[n], sibling)
-        pair.start()
-        pair.wait_recv()
-        cur[...] = x - (ssend[n].astype(F32) + srecv[n].astype(F32))
+        pairs = []
+        for half in range(2):
+            at = halves[half]
+            ssend[n, at] = (change[half] + spread(other, half, its_half)).astype(BF16)
+            pair = remote(
+                ssend.at[n, at], srecv.at[n, at], ss_sem.at[n, half], sr_sem.at[n, half], sibling
+            )
+            pair.start()
+            pairs.append(pair)
+        for half in range(2):
+            at = halves[half]
+            pairs[half].wait_recv()
+            cur[at] = cur[at] - (ssend[n, at].astype(F32) + srecv[n, at].astype(F32))
+            if n == 0:
+                term = project(half, its_half)
+                theirs = term if half == 0 else theirs + term
+            else:
+                fbuf[y, at] = cur[at].astype(BF16)
+                for j in (2, 1, 3):
+                    send = remote(
+                        fbuf.at[y, at], fbuf.at[y, at],
+                        fs_sem.at[j - 1, half], fr_sem.at[j - 1, half], along_y(j),
+                    )
+                    send.start()
+                    final.append(send)
         cross.wait_send()
         for send in sends:
             send.wait_send()
         cross_back.wait_send()
-        pair.wait_send()
-
-    fbuf[y] = cur[...].astype(BF16)
-    final = [
-        remote(fbuf.at[y], fbuf.at[y], fs_sem.at[j - 1], fr_sem.at[j - 1], along_y(j))
-        for j in (1, 2, 3)
-    ]
-    for send in final:
-        send.start()
+        for pair in pairs:
+            pair.wait_send()
+
     ebuf[1, y] = ebuf[0, 0]
     for j in (1, 2, 3):
         source = ring(j)
@@ -406,9 +429,12 @@
         coef_ref[part] = jnp.concatenate([ebuf[1, q, rows] for q in range(4)], axis=0)
     for j in (1, 2, 3):
         source = ring(4 - j)
-        remote(
-            fbuf.at[source], fbuf.at[source], fs_sem.at[j - 1], fr_sem.at[j - 1], along_y(j)
-        ).wait_recv()
+        for half in range(2):
+            at = halves[half]
+            remote(
+                fbuf.at[source, at], fbuf.at[source, at],
+                fs_sem.at[j - 1, half], fr_sem.at[j - 1, half], along_y(j),
+            ).wait_recv()
     for send in final:
         send.wait_send()
     out_ref[...] = fbuf[...]
@@ -429,6 +455,7 @@
         out_specs=(here, here),
         scratch_shapes=[
             vmem((SITES, QUARTER, 2, NB), BF16),
+            vmem((SITES, 2, NB, NB), BF16),
             vmem((SITES, 2, NB, NB), BF16),
             vmem((SITES, 2, NB, NB), BF16),
             vmem((SITES, 2, NB, NB), BF16),
@@ -456,8 +483,8 @@
             dma((3,)), dma((3,)),
             dma((2,)), dma((2,)),
             dma((2, CHIPS)), dma((2, CHIPS)),
-            dma((2,)), dma((2,)), dma((2,)), dma((2,)),
-            dma((3,)), dma((3,)), dma((3,)), dma((3,)),
+            dma((2,)), dma((2,)), dma((2, 2)), dma((2, 2)),
+            dma((3, 2)), dma((3, 2)), dma((3,)), dma((3,)),
             pltpu.SemaphoreType.REGULAR((4, 2)),
         ],
         compiler_params=pltpu.CompilerParams(

time: 81.7 us -> 79.3 us (0.971)
  Pallas kernels: 79.5 us -> 77.2 us
    pallas_call x1, Pallas kernels: 79.5 us -> 77.2 us  [shards(): pl.pallas_call(kernel, out_shape=(jax.ShapeDtypeStruct((4,) + block, BF16...]
where the time goes in v6:
time: 79.3 us
  Pallas kernels  77.2 us (97%)
  local copies, waits for them, and re-layouts  1.4 us (2%)
    pallas_call x1, Pallas kernels, shards(): pl.pallas_call(kernel, out_shape=(jax.ShapeDtypeStruct((4,) + block, BF16...  77.2 us

profile of v6, /device:TPU:1, one launch (start us, length us, event | category | flops | bytes accessed | tf_op | source)
XLA Modules:
  0.0 79.3 jit_solution(2701836177547582906)
XLA Ops:
  0.6 77.2 %shard_map.59 = (bf16[4,32,400]{2,1,0:T(8,128)(2,1)S(1)}, f32[2,16,128]{2,1,0:T(8,128)S(1)}) custom-call(bf16[4,16,2,400]{3,2,1,0:T(2,128)(2,1)} %bitcast.14, bf16[4,2,400,400]{3,2,1,0:T(8,128)(2,1)} %bitcast.11, bf16[4,2,2,400,400]{4,3,2,1,0:T(8,128)(2,1)} %bitcast.10, bf16[3200,128]{1,0:T(8,128)(2,1)} %bitcast.12), custom_call_target="tpu_custom_call" | custom-call | tf_op jit(solution)/shard_map/pallas_call | solution.py:448
  77.9 0.8 copy.6
  78.7 0.6 copy.8
  (1 shorter events, 0.0 us)

commit v7 on v6

--- a/solution.py
+++ b/solution.py
@@ -98,18 +98,27 @@
             [apply(pairs[q], time_w, 2 * half + q) for q in range(2)], axis=0
         ).astype(BF16)
 
-    loads = [
-        pltpu.make_async_copy(hop_hbm.at[:, 1], time_w, load_sem.at[0]),
-        pltpu.make_async_copy(self_hbm, self_w, load_sem.at[1]),
-        pltpu.make_async_copy(hop_hbm.at[:, 0], space_w, load_sem.at[2]),
-        pltpu.make_async_copy(stored_hbm, stored.at[:, pl.ds(0, GROUP)], load_sem.at[3]),
-        pltpu.make_async_copy(
-            start_hbm.at[:, pl.ds(y * QUARTER, QUARTER)], start, load_sem.at[4]
-        ),
+    first_load = pltpu.make_async_copy(
+        start_hbm.at[:, pl.ds(y * QUARTER, QUARTER)], start, load_sem.at[3 * SITES]
+    )
+    last_load = pltpu.make_async_copy(
+        stored_hbm, stored.at[:, pl.ds(0, GROUP)], load_sem.at[3 * SITES + 1]
+    )
+    time_loads = [
+        pltpu.make_async_copy(hop_hbm.at[q, 1], time_w.at[q], load_sem.at[q])
+        for q in range(SITES)
     ]
-    for q in (4, 0, 2, 1, 3):
-        loads[q].start()
-    loads[4].wait()
+    space_loads = [
+        pltpu.make_async_copy(hop_hbm.at[q, 0], space_w.at[q], load_sem.at[SITES + q])
+        for q in range(SITES)
+    ]
+    self_loads = [
+        pltpu.make_async_copy(self_hbm.at[q], self_w.at[q], load_sem.at[2 * SITES + q])
+        for q in range(SITES)
+    ]
+    for load in [first_load] + time_loads + space_loads + self_loads + [last_load]:
+        load.start()
+    first_load.wait()
     block = start[...].astype(F32)
     block = jnp.concatenate(
         [block[s, r, c : c + 1] for s in range(SITES) for c in range(2) for r in range(QUARTER)],
@@ -118,30 +127,22 @@
     cur[...] = block
     prev[...] = block
     psend[1] = jnp.zeros_like(psend[1])
-    loads[0].wait()
-
-    for half in range(2):
-        product(half, 0)
-
     def unit(n):
         row = lax.broadcasted_iota(jnp.int32, (n, n), 0)
         return (row == lax.broadcasted_iota(jnp.int32, (n, n), 1)).astype(BF16)
 
-    def flip(weight, flipped, by_product):
-        for site in range(SITES):
-            for part in range(2):
-                source = weight[site, part]
-                if (site, part) in by_product:
-                    value = jnp.concatenate(
-                        [dot_t(unit(256), source[:, :256]), dot_t(unit(144), source[:, 256:])], axis=0
-                    ).astype(BF16)
-                else:
-                    value = jnp.transpose(source)
-                flipped[site, part] = -value if part else value
-
-    flip(time_w, ahead_w, ((1, 0), (3, 0)))
-    loads[2].wait()
-    flip(space_w, beside_w, ((0, 1), (1, 1), (2, 1)))
+    def flip(weight, flipped, site):
+        source = weight[site, 0]
+        flipped[site, 0] = jnp.concatenate(
+            [dot_t(unit(256), source[:, :256]), dot_t(unit(144), source[:, 256:])], axis=0
+        ).astype(BF16)
+        flipped[site, 1] = -jnp.transpose(weight[site, 1])
+
+    for site in range(SITES):
+        time_loads[site].wait()
+        if site % 2:
+            product(site // 2, 0)
+        flip(time_w, ahead_w, site)
     pl.semaphore_wait(barrier, len(greet))
 
     gathers = [
@@ -278,8 +279,8 @@
 
             @pl.when(i < last)
             def _(half=half):
+                next_product(half, i)
                 send_behind(half, lax.rem(i + 1, 3), cur[halves[half]])
-                next_product(half, i)
 
     bsend[...] = cur[...].astype(BF16)
     for half in range(2):
@@ -287,7 +288,11 @@
         to_ahead(0, 0, half).start()
     for gather in gathers:
         gather.start()
-    loads[1].wait()
+    for site in range(SITES):
+        space_loads[site].wait()
+        flip(space_w, beside_w, site)
+    for load in self_loads:
+        load.wait()
 
     @pl.when(even)
     def _():
@@ -305,7 +310,7 @@
         to_ahead(0, 0, half).wait_send()
         to_ahead(1, 0, half).wait_send()
 
-    loads[3].wait()
+    last_load.wait()
     for gather in gathers:
         gather.wait()
 
@@ -478,7 +483,7 @@
             vmem((2,) + block, BF16),
             vmem((4,) + block, BF16),
             vmem((2, 4, ROWS, GROUP), F32),
-            dma((5,)),
+            dma((3 * SITES + 2,)),
             dma((2,)), dma((3, 2)), dma((2, 2)), dma((3, 2)),
             dma((3,)), dma((3,)),
             dma((2,)), dma((2,)),

time: 79.3 us -> 77.9 us (0.982)
  Pallas kernels: 77.2 us -> 75.8 us
    pallas_call x1, Pallas kernels: 77.2 us -> 75.8 us  [shards(): pl.pallas_call(kernel, out_shape=(jax.ShapeDtypeStruct((4,) + block, BF16...]
where the time goes in v7:
time: 77.9 us
  Pallas kernels  75.8 us (97%)
  local copies, waits for them, and re-layouts  1.4 us (2%)
    pallas_call x1, Pallas kernels, shards(): pl.pallas_call(kernel, out_shape=(jax.ShapeDtypeStruct((4,) + block, BF16...  75.8 us

profile of v7, /device:TPU:1, one launch (start us, length us, event | category | flops | bytes accessed | tf_op | source)
XLA Modules:
  0.0 77.9 jit_solution(2256428240921067988)
XLA Ops:
  0.6 75.8 %shard_map.59 = (bf16[4,32,400]{2,1,0:T(8,128)(2,1)S(1)}, f32[2,16,128]{2,1,0:T(8,128)S(1)}) custom-call(bf16[4,16,2,400]{3,2,1,0:T(2,128)(2,1)} %bitcast.14, bf16[4,2,400,400]{3,2,1,0:T(8,128)(2,1)} %bitcast.11, bf16[4,2,2,400,400]{4,3,2,1,0:T(8,128)(2,1)} %bitcast.10, bf16[3200,128]{1,0:T(8,128)(2,1)} %bitcast.12), custom_call_target="tpu_custom_call" | custom-call | tf_op jit(solution)/shard_map/pallas_call | solution.py:453
  76.5 0.8 copy.6
  77.2 0.6 copy.8
  (1 shorter events, 0.0 us)

commit v8 on v7

--- a/solution.py
+++ b/solution.py
@@ -282,12 +282,12 @@
                 next_product(half, i)
                 send_behind(half, lax.rem(i + 1, 3), cur[halves[half]])
 
+    for q in (1, 0, 2):
+        gathers[q].start()
     bsend[...] = cur[...].astype(BF16)
     for half in range(2):
         to_behind(0, half).start()
         to_ahead(0, 0, half).start()
-    for gather in gathers:
-        gather.start()
     for site in range(SITES):
         space_loads[site].wait()
         flip(space_w, beside_w, site)

time: 77.9 us -> 78.3 us (level)
  no operation moved by 1% of the time
where the time goes in v8:
time: 78.3 us; the launch traced here: 78.2 us
  Pallas kernels  76.2 us (97%)
  local copies, waits for them, and re-layouts  1.4 us (2%)
    pallas_call x1, Pallas kernels, shards(): pl.pallas_call(kernel, out_shape=(jax.ShapeDtypeStruct((4,) + block, BF16...  76.2 us

profile of v8, /device:TPU:1, one launch (start us, length us, event | category | flops | bytes accessed | tf_op | source)
XLA Modules:
  0.0 78.2 jit_solution(14784964847698559193)
XLA Ops:
  0.6 76.2 %shard_map.59 = (bf16[4,32,400]{2,1,0:T(8,128)(2,1)S(1)}, f32[2,16,128]{2,1,0:T(8,128)S(1)}) custom-call(bf16[4,16,2,400]{3,2,1,0:T(2,128)(2,1)} %bitcast.14, bf16[4,2,400,400]{3,2,1,0:T(8,128)(2,1)} %bitcast.11, bf16[4,2,2,400,400]{4,3,2,1,0:T(8,128)(2,1)} %bitcast.10, bf16[3200,128]{1,0:T(8,128)(2,1)} %bitcast.12), custom_call_target="tpu_custom_call" | custom-call | tf_op jit(solution)/shard_map/pallas_call | solution.py:453
  76.9 0.8 copy.6
  77.6 0.6 copy.8
  (1 shorter events, 0.0 us)
